TPU v7x, 256 devices: a whole 4x4x8 slice. The times are simulated.
256 devices in a mesh: modes: 8 (over y, core), elems: 32 (over z, x).
Axes of the slice: x: 4, y: 4, z: 8, core: 2. Of those that a mesh axis runs over, the one named last changes fastest.
Arguments:
- adjoint_modes: float32 [3, 512, 41472], P(None, 'modes', 'elems'), may hold values from -3 to 3
- base_planes: float32 [3, 8, 5184, 512], P(None, 'modes', 'elems'), may hold values from -8 to 8
- metrics: float32 [4, 512], P(None, 'elems'), may hold values from -0.12 to 0.12
- send_point: int32 [32, 32, 64], P('elems'), may hold values from 0 to 1295
- dest_node: int32 [32, 32, 64], P('elems'), may hold values from 0 to 511
- pair_counts: int32 [32, 32], P('elems'), may hold values from 0 to 64, as said below
Outputs:
- advection: float32 [3, 512, 41472], P(None, 'modes', 'elems')
- shared_totals: float32 [3, 512, 16384], P(None, 'modes', 'elems')
Inputs may be any that keep to these rules, and one draw needn't show every extreme that they name: `send_point`: a point of the source partition, numbered within its 16 elements. `pair_counts`: in every draw some owner gets 64 live slots from every source partition.
All inputs are finite; a program needn't handle non-finite values.
Results may differ from a plain program's by a relative error of at most 0.0003.
Values sent between devices are 32-bit elements; how exact they have to be, the bound alone decides.
A program may use at most 128 MiB of HBM per device.

v0:
```python
import jax
import jax.numpy as jnp
import numpy as np
from jax import lax
from jax.experimental import pallas as pl
from jax.experimental.pallas import tpu as pltpu
from jax.sharding import PartitionSpec as P

NP = 9
NODES_OWN = 512
MESH = pl.DeviceIdType.MESH
F32 = jnp.float32
BF16 = jnp.bfloat16

span_wavenumber = 0.4


def chebyshev_table(count):
    degree = count - 1
    position = np.arange(count)
    node_x = np.cos(np.pi * position / degree)
    weights = np.where((position == 0) | (position == degree), 2.0, 1.0)
    sign_terms = (-1.0) ** position
    identity = np.eye(count)
    spacing = node_x[:, None] - node_x[None, :] + identity
    matrix = (
        weights[:, None] * sign_terms[:, None] / (weights[None, :] * sign_terms[None, :]) / spacing
    )
    matrix = matrix * (1.0 - identity)
    matrix = matrix - identity * matrix.sum(axis=1)[:, None]
    return matrix


def spectral_tables(planes):
    position = np.arange(planes)
    wavenumber = np.where(position == 1, planes // 2, position // 2)
    angles = 2.0 * np.pi / planes * (position[:, None] * wavenumber[None, :] % planes)
    sine_col = (position % 2 == 1) & (position != 1)
    synth_table = np.where(sine_col[None, :], np.sin(angles), np.cos(angles))
    weighting = np.where(position <= 1, 1.0, 2.0) / planes
    analysis = synth_table.T * weighting[:, None]
    speeds = span_wavenumber * wavenumber
    slope_table = np.where(
        position[None, :] <= 1,
        0.0,
        np.where(
            sine_col[None, :], speeds[None, :] * np.cos(angles), -speeds[None, :] * np.sin(angles)
        ),
    )
    return synth_table, analysis, slope_table, slope_table @ analysis


def halves_of(table):
    single = table.astype(np.float32)
    high = single.astype(BF16)
    low = (single - high.astype(np.float32)).astype(BF16)
    return high, low


def gradient_tables(sub_elems, width):
    diff = chebyshev_table(NP)
    points = sub_elems * NP * NP
    tables = np.zeros((2, width, width), np.float32)
    along = (np.kron(diff, np.eye(NP)), np.kron(np.eye(NP), diff))
    for direction in range(2):
        for elem in range(sub_elems):
            rows = slice(elem * NP * NP, (elem + 1) * NP * NP)
            tables[direction, rows, rows] = along[direction].T
    assert points <= width
    return tables


def split(value):
    high = value.astype(BF16)
    return high, (value - high.astype(F32)).astype(BF16)


def dot(left, right):
    return jnp.dot(left, right, preferred_element_type=F32)


def dot3(left_high, left_low, right_high, right_low):
    return dot(left_high, right_high) + (dot(left_high, right_low) + dot(left_low, right_high))


def dot6(left, right):
    return jnp.dot(left, right, precision=lax.Precision.HIGHEST, preferred_element_type=F32)


def body(
    groups,
    partners,
    points,
    x_hbm,
    base_hbm,
    metrics,
    picks,
    nodes,
    synth_high_hbm,
    synth_low_hbm,
    dz_hbm,
    analysis_high_hbm,
    analysis_low_hbm,
    grad_hbm,
    advection_hbm,
    totals_hbm,
    x_v,
    base_v,
    synth_high,
    synth_low,
    dz,
    analysis_high,
    analysis_low,
    grad_tables,
    stage_a,
    stage_b,
    coef_a,
    coef_b,
    padded,
    base_t,
    base_z,
    flow_xy,
    grad_high,
    grad_low,
    pick_table,
    node_rows,
    node_table,
    node_in,
    vel,
    along_z,
    vel_xy,
    phys_high,
    phys_low,
    adv,
    send_adv,
    recv_adv,
    advection,
    adv_parts,
    send_slots,
    recv_slots,
    slot_parts,
    totals,
    load_sem,
    store_sem,
    a_send,
    a_recv,
    b_send,
    b_recv,
    adv_send,
    adv_recv,
    node_send,
    node_recv,
    slot_send,
    slot_recv,
):
    me = lax.axis_index("modes")
    part = lax.axis_index("elems")
    planes = dz.shape[0]
    coefs = planes // groups
    extra = points - 128
    pairs = partners // 2
    full = groups * points

    loads = [
        pltpu.make_async_copy(source, target, load_sem.at[i])
        for i, (source, target) in enumerate(
            (
                (x_hbm, x_v),
                (base_hbm, base_v),
                (grad_hbm, grad_tables),
                (dz_hbm, dz),
                (synth_high_hbm, synth_high),
                (synth_low_hbm, synth_low),
                (analysis_high_hbm, analysis_high),
                (analysis_low_hbm, analysis_low),
            )
        )
    ]
    for load in loads:
        load.start()

    barrier = pltpu.get_barrier_semaphore()

    def group_peer(d):
        return lax.rem(me + d, groups)

    def part_peer(d):
        return lax.rem(part + d, partners)

    def greet_group(d, carry):
        pl.semaphore_signal(barrier, inc=1, device_id=(group_peer(d), part), device_id_type=MESH)
        return carry

    def greet_part(d, carry):
        pl.semaphore_signal(barrier, inc=1, device_id=(me, part_peer(d)), device_id_type=MESH)
        return carry

    lax.fori_loop(1, groups, greet_group, 0)
    lax.fori_loop(1, partners, greet_part, 0)

    loads[0].wait()
    for g in range(groups):
        first = g * points
        stage_a[g, :, 0:128] = x_v[0, :, first : first + 128]
        stage_a[g, :, 128:256] = x_v[1, :, first : first + 128]
        stage_b[g, :, 0:128] = x_v[2, :, first : first + 128]
        rest = [x_v[c, :, first + 128 : first + points] for c in range(3)]
        rest.append(jnp.zeros((coefs, 128 - 3 * extra), F32))
        stage_b[g, :, 128:256] = jnp.concatenate(rest, axis=1)

    pl.semaphore_wait(barrier, groups - 1 + partners - 1)

    def group_copy(source, target, send, recv, to, slot):
        return pltpu.make_async_remote_copy(
            src_ref=source,
            dst_ref=target,
            send_sem=send.at[slot],
            recv_sem=recv.at[me],
            device_id=(to, part),
            device_id_type=MESH,
        )

    def group_arrival(target, send, recv, origin):
        return pltpu.make_async_remote_copy(
            src_ref=target,
            dst_ref=target,
            send_sem=send.at[origin],
            recv_sem=recv.at[origin],
            device_id=(origin, part),
            device_id_type=MESH,
        )

    def send_a(d, carry):
        to = group_peer(d)
        group_copy(stage_a.at[to], coef_a.at[me], a_send, a_recv, to, to).start()
        return carry

    def send_b(d, carry):
        to = group_peer(d)
        group_copy(stage_b.at[to], coef_b.at[me], b_send, b_recv, to, to).start()
        return carry

    lax.fori_loop(1, groups, send_a, 0)
    lax.fori_loop(1, groups, send_b, 0)
    coef_a[me] = stage_a[me]
    coef_b[me] = stage_b[me]

    def part_copy(source, target, send, recv, to):
        return pltpu.make_async_remote_copy(
            src_ref=source,
            dst_ref=target,
            send_sem=send.at[to],
            recv_sem=recv.at[part],
            device_id=(me, to),
            device_id_type=MESH,
        )

    def part_arrival(target, send, recv, origin):
        return pltpu.make_async_remote_copy(
            src_ref=target,
            dst_ref=target,
            send_sem=send.at[origin],
            recv_sem=recv.at[origin],
            device_id=(me, origin),
            device_id_type=MESH,
        )

    def send_nodes(d, carry):
        to = part_peer(d)
        part_copy(nodes.at[to], node_in.at[part], node_send, node_recv, to).start()
        return carry

    lax.fori_loop(1, partners, send_nodes, 0)
    node_in[part] = nodes[part]

    loads[1].wait()
    loads[2].wait()
    loads[3].wait()
    lane_points = lax.broadcasted_iota(jnp.int32, (1, 256), 1)
    first_elem = me * (points // (NP * NP))

    def metric_row(r):
        row = jnp.zeros((1, 256), F32)
        for e in range(points // (NP * NP)):
            row = jnp.where(lane_points >= e * NP * NP, metrics[r, first_elem + e], row)
        return row

    for half in range(2):
        grad = grad_tables[0] * metric_row(2 * half) + grad_tables[1] * metric_row(2 * half + 1)
        high, low = split(grad)
        grad_high[:, half * 256 : half * 256 + 256] = high
        grad_low[:, half * 256 : half * 256 + 256] = low
        vel_xy[0, 0:256, half * 256 : half * 256 + 256] = grad
    padded[128:256, :] = jnp.zeros((128, planes), F32)

    def base_step(c, carry):
        padded[0:points, :] = base_v[c, 0]
        base_t[c] = jnp.transpose(padded[...])
        base_z[c] = dot6(dz[...], base_t[c])
        flow_xy[c] = dot6(base_t[c], vel_xy[0, 0:256, :])
        return carry

    lax.fori_loop(0, 3, base_step, 0)

    rows = pick_table.shape[0]
    point_idx = lax.broadcasted_iota(jnp.int32, (rows, 128), 0)

    def pick_step(j, carry):
        wanted = picks[pl.ds(j, 1), :]
        columns = pl.ds(pl.multiple_of(j * 128, 128), 128)
        pick_table[:, columns] = jnp.where(point_idx == wanted, 1.0, 0.0).astype(BF16)
        return carry

    lax.fori_loop(0, pairs, pick_step, 0)

    def wait_nodes(d, carry):
        origin = part_peer(d)
        part_arrival(node_in.at[origin], node_send, node_recv, origin).wait_recv()
        return carry

    lax.fori_loop(1, partners, wait_nodes, 0)
    lane = lax.broadcasted_iota(jnp.int32, (1, 128), 1)
    left = lane < 64
    node_rows[...] = jnp.zeros((128, 128), F32)
    for j in range(pairs):
        node_rows[j : j + 1, :] = jnp.where(left, node_in[2 * j], node_in[2 * j + 1])
    node_columns = jnp.transpose(node_rows[...])
    node_idx = lax.broadcasted_iota(jnp.int32, (128, NODES_OWN), 1).astype(F32)
    for j in range(pairs):
        node_table[128 * j : 128 * j + 128, :] = jnp.where(
            node_idx == node_columns[:, j : j + 1], 1.0, 0.0
        ).astype(BF16)
    adv_parts[:, rows - 128 : rows] = jnp.zeros((2 * coefs, 128), BF16)

    for load in loads[4:]:
        load.wait()

    def wait_a(d, carry):
        origin = group_peer(d)
        group_arrival(coef_a.at[origin], a_send, a_recv, origin).wait_recv()
        return carry

    lax.fori_loop(1, groups, wait_a, 0)
    high, low = split(coef_a[...].reshape(planes, 256))
    both = dot3(synth_high[...], synth_low[...], high, low)
    vel[0, :, 0:128] = both[0:planes, 0:128]
    vel[1, :, 0:128] = both[0:planes, 128:256]
    along_z[0, :, 0:128] = both[planes : 2 * planes, 0:128]
    along_z[1, :, 0:128] = both[planes : 2 * planes, 128:256]

    def wait_b(d, carry):
        origin = group_peer(d)
        group_arrival(coef_b.at[origin], b_send, b_recv, origin).wait_recv()
        return carry

    lax.fori_loop(1, groups, wait_b, 0)
    high, low = split(coef_b[...].reshape(planes, 256))
    both = dot3(synth_high[...], synth_low[...], high, low)
    vel[2, :, 0:128] = both[0:planes, 0:128]
    along_z[2, :, 0:128] = both[planes : 2 * planes, 0:128]
    for c in range(3):
        rest = both[:, 128:256]
        if c:
            rest = pltpu.roll(rest, 128 - c * extra, 1)
        rest = jnp.where(lane < extra, rest, 0.0)
        vel[c, :, 128:256] = rest[0:planes]
        along_z[c, :, 128:256] = rest[planes : 2 * planes]

    def grad_step(c, carry):
        high, low = split(vel[c])
        vel_xy[c] = dot3(high, low, grad_high[...], grad_low[...])
        return carry

    lax.fori_loop(0, 3, grad_step, 0)

    block = 32
    packed = 24

    for i in range(3):

        def point_step(b, carry, i=i):
            at = pl.ds(pl.multiple_of(b * block, block), block)
            total = jnp.zeros((block, 256), F32)
            for j in range(3):
                slope = along_z[i, at, :] if j == 2 else vel_xy[i, at, j * 256 : j * 256 + 256]
                back = base_z[j, at, :] if i == 2 else flow_xy[j, at, i * 256 : i * 256 + 256]
                total = total - base_t[j, at, :] * slope + vel[j, at, :] * back
            high, low = split(total)
            phys_high[at, :] = high
            phys_low[at, :] = low
            return carry

        lax.fori_loop(0, planes // block, point_step, 0)
        adv[...] = dot3(analysis_high[...], analysis_low[...], phys_high[...], phys_low[...])
        for m in range(groups):
            send_adv[i, m, 0:coefs, :] = adv[m * coefs : (m + 1) * coefs, 0:128]
            rest = adv[m * coefs : (m + 1) * coefs, 128:256]
            second = pltpu.roll(rest[packed : 2 * packed], extra, 1)
            third = pltpu.roll(
                jnp.concatenate([rest[2 * packed :], rest[: 3 * packed - coefs]], axis=0),
                2 * extra,
                1,
            )
            send_adv[i, m, coefs : coefs + packed, :] = jnp.where(
                lane < extra, rest[:packed], jnp.where(lane < 2 * extra, second, third)
            )

        def send_back(d, carry, i=i):
            to = group_peer(d)
            group_copy(
                send_adv.at[i, to], recv_adv.at[i, me], adv_send.at[i], adv_recv.at[i], to, to
            ).start()
            return carry

        lax.fori_loop(1, groups, send_back, 0)
        recv_adv[i, me] = send_adv[i, me]

    stores = []
    for i in range(3):

        def wait_back(d, carry, i=i):
            origin = group_peer(d)
            group_arrival(
                recv_adv.at[i, origin], adv_send.at[i], adv_recv.at[i], origin
            ).wait_recv()
            return carry

        lax.fori_loop(1, groups, wait_back, 0)
        for g in range(groups):
            first = g * points
            rest = recv_adv[i, g, coefs : coefs + packed, :]
            rest = jnp.concatenate(
                [
                    rest,
                    pltpu.roll(rest, 128 - extra, 1),
                    pltpu.roll(rest, 128 - 2 * extra, 1)[: coefs - 2 * packed],
                ],
                axis=0,
            )
            advection[i, :, first : first + 128] = recv_adv[i, g, 0:coefs, :]
            advection[i, :, first + 128 : first + points] = rest[:, :extra]
        store = pltpu.make_async_copy(advection.at[i], advection_hbm.at[i], store_sem.at[i])
        store.start()
        stores.append(store)
        high, low = split(advection[i])
        adv_parts[0:coefs, 0:full] = high
        adv_parts[coefs : 2 * coefs, 0:full] = low
        half = coefs // 2
        wide = min(512, 128 * pairs)
        for tile in range(128 * pairs // wide):
            picked = dot(adv_parts[...], pick_table[:, tile * wide : (tile + 1) * wide])
            picked = picked[0:coefs] + picked[coefs : 2 * coefs]
            for j in range(wide // 128):
                upper = picked[0:half, j * 128 : j * 128 + 128]
                lower = picked[half:coefs, j * 128 : j * 128 + 128]
                owner = 2 * (tile * (wide // 128) + j)
                send_slots[i, owner] = jnp.where(left, upper, pltpu.roll(lower, 64, 1))
                send_slots[i, owner + 1] = jnp.where(left, pltpu.roll(upper, 64, 1), lower)

        def send_picked(d, carry, i=i):
            to = part_peer(d)
            part_copy(
                send_slots.at[i, to], recv_slots.at[i, part], slot_send.at[i], slot_recv.at[i], to
            ).start()
            return carry

        lax.fori_loop(1, partners, send_picked, 0)
        recv_slots[i, part] = send_slots[i, part]

    for i in range(3):

        def wait_picked(d, carry, i=i):
            origin = part_peer(d)
            part_arrival(
                recv_slots.at[i, origin], slot_send.at[i], slot_recv.at[i], origin
            ).wait_recv()
            return carry

        lax.fori_loop(1, partners, wait_picked, 0)
        half = coefs // 2
        for j in range(pairs):
            even = recv_slots[i, 2 * j]
            odd = recv_slots[i, 2 * j + 1]
            upper = jnp.where(left, even, pltpu.roll(odd, 64, 1))
            lower = jnp.where(left, pltpu.roll(even, 64, 1), odd)
            high, low = split(jnp.concatenate([upper, lower], axis=0))
            slot_parts[0:coefs, j * 128 : j * 128 + 128] = high
            slot_parts[coefs : 2 * coefs, j * 128 : j * 128 + 128] = low
        summed = dot(slot_parts[...], node_table[...])
        totals[i] = summed[0:coefs] + summed[coefs : 2 * coefs]
        store = pltpu.make_async_copy(totals.at[i], totals_hbm.at[i], store_sem.at[3 + i])
        store.start()
        stores.append(store)

    def sent_group(d, carry):
        to = group_peer(d)
        group_copy(stage_a.at[to], coef_a.at[me], a_send, a_recv, to, to).wait_send()
        group_copy(stage_b.at[to], coef_b.at[me], b_send, b_recv, to, to).wait_send()
        for i in range(3):
            group_copy(
                send_adv.at[i, to], recv_adv.at[i, me], adv_send.at[i], adv_recv.at[i], to, to
            ).wait_send()
        return carry

    lax.fori_loop(1, groups, sent_group, 0)

    def sent_part(d, carry):
        to = part_peer(d)
        part_copy(nodes.at[to], node_in.at[part], node_send, node_recv, to).wait_send()
        for i in range(3):
            part_copy(
                send_slots.at[i, to], recv_slots.at[i, part], slot_send.at[i], slot_recv.at[i], to
            ).wait_send()
        return carry

    lax.fori_loop(1, partners, sent_part, 0)
    for store in stores:
        store.wait()


def per_device(adjoint_modes, base_planes, metrics, send_point, dest_node, pair_counts):
    components, coefs, local_points = adjoint_modes.shape
    planes = base_planes.shape[3]
    groups = lax.axis_size("modes")
    partners = lax.axis_size("elems")
    points = local_points // groups
    pairs = partners // 2
    slot_count = send_point.shape[2]
    synth, analysis, slope, dz = spectral_tables(planes)
    synth_high, synth_low = halves_of(np.concatenate([synth, slope], axis=0))
    analysis_high, analysis_low = halves_of(analysis)
    grad = gradient_tables(points // (NP * NP), 256)

    live = jnp.arange(slot_count, dtype=jnp.int32)[None, :] < pair_counts[0][:, None]
    picks = jnp.where(live, send_point[0], -1).reshape(pairs, 2 * slot_count)
    nodes = jnp.where(live, dest_node[0], -1).astype(F32)
    nodes = jnp.concatenate([nodes, nodes], axis=1)[:, None, :]

    rows = -(-local_points // 128) * 128
    any_spec = pl.BlockSpec(memory_space=pl.ANY)
    vmem_spec = pl.BlockSpec(memory_space=pltpu.VMEM)
    smem_spec = pl.BlockSpec(memory_space=pltpu.SMEM)

    def room(*shape, dtype=F32):
        return pltpu.VMEM(shape, dtype)

    dma = pltpu.SemaphoreType.DMA
    scratch = [
        room(3, coefs, local_points),
        room(3, 1, points, planes),
        room(2 * planes, planes, dtype=BF16),
        room(2 * planes, planes, dtype=BF16),
        room(planes, planes),
        room(planes, planes, dtype=BF16),
        room(planes, planes, dtype=BF16),
        room(2, 256, 256),
        room(groups, coefs, 256),
        room(groups, coefs, 256),
        room(groups, coefs, 256),
        room(groups, coefs, 256),
        room(256, planes),
        room(3, planes, 256),
        room(3, planes, 256),
        room(3, planes, 512),
        room(256, 512, dtype=BF16),
        room(256, 512, dtype=BF16),
        room(rows, pairs * 128, dtype=BF16),
        room(128, 128),
        room(pairs * 128, NODES_OWN, dtype=BF16),
        room(partners, 1, 128),
        room(3, planes, 256),
        room(3, planes, 256),
        room(3, planes, 512),
        room(planes, 256, dtype=BF16),
        room(planes, 256, dtype=BF16),
        room(planes, 256),
        room(3, groups, coefs + 24, 128),
        room(3, groups, coefs + 24, 128),
        room(3, coefs, local_points),
        room(2 * coefs, rows, dtype=BF16),
        room(3, partners, coefs // 2, 128),
        room(3, partners, coefs // 2, 128),
        room(2 * coefs, pairs * 128, dtype=BF16),
        room(3, coefs, NODES_OWN),
        dma((8,)),
        dma((6,)),
        dma((groups,)),
        dma((groups,)),
        dma((groups,)),
        dma((groups,)),
        dma((3, groups)),
        dma((3, groups)),
        dma((partners,)),
        dma((partners,)),
        dma((3, partners)),
        dma((3, partners)),
    ]

    def kernel(*refs):
        body(groups, partners, points, *refs)

    return pl.pallas_call(
        kernel,
        out_shape=(
            jax.ShapeDtypeStruct((3, coefs, local_points), F32),
            jax.ShapeDtypeStruct((3, coefs, NODES_OWN), F32),
        ),
        in_specs=[any_spec, any_spec, smem_spec, vmem_spec, vmem_spec] + [any_spec] * 6,
        out_specs=(any_spec, any_spec),
        scratch_shapes=scratch,
        compiler_params=pltpu.CompilerParams(
            collective_id=0, has_side_effects=True, vmem_limit_bytes=56 * 1024 * 1024
        ),
    )(
        adjoint_modes,
        base_planes,
        metrics,
        picks,
        nodes,
        synth_high,
        synth_low,
        jnp.asarray(dz, dtype=F32),
        analysis_high,
        analysis_low,
        grad,
    )


def solution(mesh):
    return jax.shard_map(
        per_device,
        mesh=mesh,
        in_specs=(
            P(None, "modes", "elems"),
            P(None, "modes", "elems", None),
            P(None, "elems"),
            P("elems", None, None),
            P("elems", None, None),
            P("elems", None),
        ),
        out_specs=(P(None, "modes", "elems"), P(None, "modes", "elems")),
        check_vma=False,
    )
```

profile of v0, /device:TPU:1, one launch (start us, length us, event | category | flops | bytes accessed | tf_op | source)
XLA Modules:
  0.0 89.9 jit_solution(13438284520318343131)
XLA Ops:
  0.6 0.5 broadcast.7
  1.1 1.3 %reduce.3 = s32[32]{0:T(128)S(1)} reduce(s32[1,32]{1,0:T(1,128)} %param.17, s32[]{:T(128)} %broadcast.7), dimensions={0}, to_apply=%param.17.reduce_sub_computation.3 | reduce | bytes 260 | tf_op args[5]
  2.5 0.1 lt.31
  2.5 0.1 lt.33
  2.6 0.1 lt.34
  2.7 0.1 lt.35
  2.8 0.8 squeeze.6
  3.6 0.6 compare_select_fusion.refs_3_
  4.2 0.8 fusion
  5.0 0.7 pad_maximum_fusion
  5.7 2.3 %copy.15.refs_1_ = f32[3,1,162,512]{3,2,1,0:T(8,128)} copy(f32[3,1,162,512]{3,1,2,0:T(1,128)} %param.13) | data formatting | bytes 1990656 | tf_op args[1]
  7.9 78.9 %shard_map.131 = (f32[3,64,1296]{2,1,0:T(8,128)}, f32[3,64,512]{2,1,0:T(8,128)}) custom-call(f32[3,64,1296]{2,1,0:T(8,128)} %refs_0_.1, f32[3,1,162,512]{3,2,1,0:T(8,128)} %copy.15.refs_1_, f32[4,16]{1,0:T(4,128)} %refs_2_.1, s32[16,128]{1,0:T(8,128)} %compare_select_fusion.refs_3_, f32[32,1,128]{2,1,0:T(1,128)} %bitcast.6, ...), custom_call_target="tpu_custom_call" | custom-call | tf_op jit(solution)/shard_map/pallas_call | solution.py:602
  86.8 0.0 copy-start
  86.8 2.3 %copy.18 = f32[3,64,1296]{2,1,0:T(8,128)} copy(f32[3,64,1296]{2,1,0:T(8,128)} %get-tuple-element.4) | data formatting | bytes 1990656
  89.1 0.0 copy-done
  89.2 0.7 copy.19
  (1 shorter events, 0.0 us)
Async XLA Ops:
  86.8 2.3 %copy-start = (f32[3,64,512]{2,1,0:T(8,128)S(1)}, f32[3,64,512]{2,1,0:T(8,128)}, u32[]{:S(2)}) copy-start(f32[3,64,512]{2,1,0:T(8,128)} %get-tuple-element.5) | copy-start | bytes 1179652
where the time goes:
time: 90.3 us; the launch traced here: 89.9 us
  Pallas kernels  78.9 us (87%)
  local copies, waits for them, and re-layouts  6.99 us (8%)
  other arithmetic  3.39 us (4%)
    pallas_call x1, Pallas kernels, per_device(): pl.pallas_call(kernel, out_shape=(jax.ShapeDtypeStruct((3, coefs, local_p...  78.9 us
    unnamed x6, local copies, waits for them, and re-layouts  5.86 us

commit v1 on v0

--- a/solution.py
+++ b/solution.py
@@ -13,6 +13,12 @@
 BF16 = jnp.bfloat16
 
 span_wavenumber = 0.4
+
+CHUNKS = ((0, 0, 16, 2), (0, 16, 48, 3), (1, 0, 64, 3), (2, 0, 64, 3))
+
+
+def packed_rows(count, fold):
+    return -(-count // (8 * fold)) * 8
 
 
 def chebyshev_table(count):
@@ -93,9 +99,10 @@
     points,
     x_hbm,
     base_hbm,
-    metrics,
-    picks,
-    nodes,
+    metrics_hbm,
+    send_point_hbm,
+    dest_node_hbm,
+    pair_counts_hbm,
     synth_high_hbm,
     synth_low_hbm,
     dz_hbm,
@@ -106,6 +113,10 @@
     totals_hbm,
     x_v,
     base_v,
+    metrics,
+    send_point,
+    dest_node,
+    pair_counts,
     synth_high,
     synth_low,
     dz,
@@ -122,6 +133,8 @@
     flow_xy,
     grad_high,
     grad_low,
+    picks,
+    nodes,
     pick_table,
     node_rows,
     node_table,
@@ -132,12 +145,8 @@
     phys_high,
     phys_low,
     adv,
-    send_adv,
-    recv_adv,
     advection,
     adv_parts,
-    send_slots,
-    recv_slots,
     slot_parts,
     totals,
     load_sem,
@@ -152,7 +161,11 @@
     node_recv,
     slot_send,
     slot_recv,
+    *chunk_rooms,
 ):
+    send_adv, recv_adv, send_slots, recv_slots = (
+        chunk_rooms[i * len(CHUNKS) : (i + 1) * len(CHUNKS)] for i in range(4)
+    )
     me = lax.axis_index("modes")
     part = lax.axis_index("elems")
     planes = dz.shape[0]
@@ -161,11 +174,34 @@
     pairs = partners // 2
     full = groups * points
 
+    barrier = pltpu.get_barrier_semaphore()
+
+    def group_peer(d):
+        return lax.rem(me + d, groups)
+
+    def part_peer(d):
+        return lax.rem(part + d, partners)
+
+    def greet_group(d, carry):
+        pl.semaphore_signal(barrier, inc=1, device_id=(group_peer(d), part), device_id_type=MESH)
+        return carry
+
+    def greet_part(d, carry):
+        pl.semaphore_signal(barrier, inc=1, device_id=(me, part_peer(d)), device_id_type=MESH)
+        return carry
+
+    lax.fori_loop(1, groups, greet_group, 0)
+    lax.fori_loop(1, partners, greet_part, 0)
+
     loads = [
         pltpu.make_async_copy(source, target, load_sem.at[i])
         for i, (source, target) in enumerate(
             (
                 (x_hbm, x_v),
+                (send_point_hbm, send_point),
+                (dest_node_hbm, dest_node),
+                (pair_counts_hbm, pair_counts),
+                (metrics_hbm, metrics),
                 (base_hbm, base_v),
                 (grad_hbm, grad_tables),
                 (dz_hbm, dz),
@@ -178,25 +214,6 @@
     ]
     for load in loads:
         load.start()
-
-    barrier = pltpu.get_barrier_semaphore()
-
-    def group_peer(d):
-        return lax.rem(me + d, groups)
-
-    def part_peer(d):
-        return lax.rem(part + d, partners)
-
-    def greet_group(d, carry):
-        pl.semaphore_signal(barrier, inc=1, device_id=(group_peer(d), part), device_id_type=MESH)
-        return carry
-
-    def greet_part(d, carry):
-        pl.semaphore_signal(barrier, inc=1, device_id=(me, part_peer(d)), device_id_type=MESH)
-        return carry
-
-    lax.fori_loop(1, groups, greet_group, 0)
-    lax.fori_loop(1, partners, greet_part, 0)
 
     loads[0].wait()
     for g in range(groups):
@@ -245,6 +262,22 @@
     coef_a[me] = stage_a[me]
     coef_b[me] = stage_b[me]
 
+    for load in loads[1:4]:
+        load.wait()
+    owner_idx = lax.broadcasted_iota(jnp.int32, (partners, 64), 0)
+    slot_idx = lax.broadcasted_iota(jnp.int32, (partners, 64), 1)
+    live = jnp.zeros((partners, 64), jnp.int32)
+    for o in range(partners):
+        live = jnp.where(owner_idx == o, pair_counts[0, o], live)
+    live = slot_idx < live
+    wanted = jnp.where(live, send_point[0], -1)
+    fed = jnp.where(live, dest_node[0], -1).astype(F32)
+    for o in range(partners):
+        side = o % 2 * 64
+        picks[o // 2 : o // 2 + 1, side : side + 64] = wanted[o : o + 1]
+        nodes[o, :, 0:64] = fed[o : o + 1]
+        nodes[o, :, 64:128] = fed[o : o + 1]
+
     def part_copy(source, target, send, recv, to):
         return pltpu.make_async_remote_copy(
             src_ref=source,
@@ -273,9 +306,8 @@
     lax.fori_loop(1, partners, send_nodes, 0)
     node_in[part] = nodes[part]
 
-    loads[1].wait()
-    loads[2].wait()
-    loads[3].wait()
+    for load in loads[4:8]:
+        load.wait()
     lane_points = lax.broadcasted_iota(jnp.int32, (1, 256), 1)
     first_elem = me * (points // (NP * NP))
 
@@ -290,14 +322,14 @@
         high, low = split(grad)
         grad_high[:, half * 256 : half * 256 + 256] = high
         grad_low[:, half * 256 : half * 256 + 256] = low
-        vel_xy[0, 0:256, half * 256 : half * 256 + 256] = grad
+        vel_xy[0:256, half * 256 : half * 256 + 256] = grad
     padded[128:256, :] = jnp.zeros((128, planes), F32)
 
     def base_step(c, carry):
-        padded[0:points, :] = base_v[c, 0]
+        padded[0:points, :] = base_v[c, :, 0, :]
         base_t[c] = jnp.transpose(padded[...])
         base_z[c] = dot6(dz[...], base_t[c])
-        flow_xy[c] = dot6(base_t[c], vel_xy[0, 0:256, :])
+        flow_xy[c] = dot6(base_t[c], vel_xy[0:256, :])
         return carry
 
     lax.fori_loop(0, 3, base_step, 0)
@@ -332,7 +364,7 @@
         ).astype(BF16)
     adv_parts[:, rows - 128 : rows] = jnp.zeros((2 * coefs, 128), BF16)
 
-    for load in loads[4:]:
+    for load in loads[8:]:
         load.wait()
 
     def wait_a(d, carry):
@@ -366,23 +398,17 @@
         vel[c, :, 128:256] = rest[0:planes]
         along_z[c, :, 128:256] = rest[planes : 2 * planes]
 
-    def grad_step(c, carry):
-        high, low = split(vel[c])
-        vel_xy[c] = dot3(high, low, grad_high[...], grad_low[...])
-        return carry
-
-    lax.fori_loop(0, 3, grad_step, 0)
-
     block = 32
-    packed = 24
-
-    for i in range(3):
-
-        def point_step(b, carry, i=i):
+
+    def advect(i):
+        high, low = split(vel[i])
+        vel_xy[...] = dot3(high, low, grad_high[...], grad_low[...])
+
+        def point_step(b, carry):
             at = pl.ds(pl.multiple_of(b * block, block), block)
             total = jnp.zeros((block, 256), F32)
             for j in range(3):
-                slope = along_z[i, at, :] if j == 2 else vel_xy[i, at, j * 256 : j * 256 + 256]
+                slope = along_z[i, at, :] if j == 2 else vel_xy[at, j * 256 : j * 256 + 256]
                 back = base_z[j, at, :] if i == 2 else flow_xy[j, at, i * 256 : i * 256 + 256]
                 total = total - base_t[j, at, :] * slope + vel[j, at, :] * back
             high, low = split(total)
@@ -392,114 +418,156 @@
 
         lax.fori_loop(0, planes // block, point_step, 0)
         adv[...] = dot3(analysis_high[...], analysis_low[...], phys_high[...], phys_low[...])
+
+    def back_copy(n, to):
+        return group_copy(
+            send_adv[n].at[to], recv_adv[n].at[me], adv_send.at[n], adv_recv.at[n], to, to
+        )
+
+    def send_back(n):
+        _, start, count, fold = CHUNKS[n]
+        packed = packed_rows(count, fold)
         for m in range(groups):
-            send_adv[i, m, 0:coefs, :] = adv[m * coefs : (m + 1) * coefs, 0:128]
-            rest = adv[m * coefs : (m + 1) * coefs, 128:256]
-            second = pltpu.roll(rest[packed : 2 * packed], extra, 1)
-            third = pltpu.roll(
-                jnp.concatenate([rest[2 * packed :], rest[: 3 * packed - coefs]], axis=0),
-                2 * extra,
-                1,
-            )
-            send_adv[i, m, coefs : coefs + packed, :] = jnp.where(
-                lane < extra, rest[:packed], jnp.where(lane < 2 * extra, second, third)
-            )
-
-        def send_back(d, carry, i=i):
-            to = group_peer(d)
-            group_copy(
-                send_adv.at[i, to], recv_adv.at[i, me], adv_send.at[i], adv_recv.at[i], to, to
-            ).start()
+            at = m * coefs + start
+            send_adv[n][m, 0:count, :] = adv[at : at + count, 0:128]
+            rest = adv[at : at + count, 128:256]
+            merged = rest[:packed]
+            for f in range(1, fold):
+                piece = rest[f * packed : min((f + 1) * packed, count)]
+                if piece.shape[0] < packed:
+                    filler = jnp.zeros((packed - piece.shape[0], 128), F32)
+                    piece = jnp.concatenate([piece, filler], axis=0)
+                merged = jnp.where(lane < f * extra, merged, pltpu.roll(piece, f * extra, 1))
+            send_adv[n][m, count : count + packed, :] = merged
+
+        def step(d, carry):
+            back_copy(n, group_peer(d)).start()
             return carry
 
-        lax.fori_loop(1, groups, send_back, 0)
-        recv_adv[i, me] = send_adv[i, me]
+        lax.fori_loop(1, groups, step, 0)
+        recv_adv[n][me] = send_adv[n][me]
 
     stores = []
-    for i in range(3):
-
-        def wait_back(d, carry, i=i):
+
+    def slot_copy(n, to):
+        return part_copy(
+            send_slots[n].at[to], recv_slots[n].at[part], slot_send.at[n], slot_recv.at[n], to
+        )
+
+    wide = min(512, 128 * pairs)
+    tiles = 128 * pairs // wide
+    tile_owners = 2 * (wide // 128)
+
+    def send_picked(n):
+        i, start, count, fold = CHUNKS[n]
+        packed = packed_rows(count, fold)
+
+        def arrive(d, carry):
             origin = group_peer(d)
             group_arrival(
-                recv_adv.at[i, origin], adv_send.at[i], adv_recv.at[i], origin
+                recv_adv[n].at[origin], adv_send.at[n], adv_recv.at[n], origin
             ).wait_recv()
             return carry
 
-        lax.fori_loop(1, groups, wait_back, 0)
+        lax.fori_loop(1, groups, arrive, 0)
         for g in range(groups):
             first = g * points
-            rest = recv_adv[i, g, coefs : coefs + packed, :]
-            rest = jnp.concatenate(
-                [
-                    rest,
-                    pltpu.roll(rest, 128 - extra, 1),
-                    pltpu.roll(rest, 128 - 2 * extra, 1)[: coefs - 2 * packed],
-                ],
-                axis=0,
-            )
-            advection[i, :, first : first + 128] = recv_adv[i, g, 0:coefs, :]
-            advection[i, :, first + 128 : first + points] = rest[:, :extra]
-        store = pltpu.make_async_copy(advection.at[i], advection_hbm.at[i], store_sem.at[i])
+            rest = recv_adv[n][g, count : count + packed, :]
+            pieces = [rest]
+            for f in range(1, fold):
+                piece = pltpu.roll(rest, 128 - f * extra, 1)
+                pieces.append(piece[: min(packed, count - f * packed)])
+            rest = jnp.concatenate(pieces, axis=0)
+            advection[i, start : start + count, first : first + 128] = recv_adv[n][g, 0:count, :]
+            advection[i, start : start + count, first + 128 : first + points] = rest[:, :extra]
+        store = pltpu.make_async_copy(
+            advection.at[i, pl.ds(start, count)],
+            advection_hbm.at[i, pl.ds(start, count)],
+            store_sem.at[n],
+        )
         store.start()
         stores.append(store)
-        high, low = split(advection[i])
-        adv_parts[0:coefs, 0:full] = high
-        adv_parts[coefs : 2 * coefs, 0:full] = low
-        half = coefs // 2
-        wide = min(512, 128 * pairs)
-        for tile in range(128 * pairs // wide):
-            picked = dot(adv_parts[...], pick_table[:, tile * wide : (tile + 1) * wide])
-            picked = picked[0:coefs] + picked[coefs : 2 * coefs]
+        high, low = split(advection[i, start : start + count, :])
+        adv_parts[0:count, 0:full] = high
+        adv_parts[count : 2 * count, 0:full] = low
+        half = count // 2
+
+        def pick(t, carry):
+            tile = lax.rem(part // tile_owners + t, tiles)
+            columns = pl.ds(pl.multiple_of(tile * wide, 128), wide)
+            picked = dot(adv_parts[0 : 2 * count, :], pick_table[:, columns])
+            picked = picked[0:count] + picked[count : 2 * count]
             for j in range(wide // 128):
                 upper = picked[0:half, j * 128 : j * 128 + 128]
-                lower = picked[half:coefs, j * 128 : j * 128 + 128]
-                owner = 2 * (tile * (wide // 128) + j)
-                send_slots[i, owner] = jnp.where(left, upper, pltpu.roll(lower, 64, 1))
-                send_slots[i, owner + 1] = jnp.where(left, pltpu.roll(upper, 64, 1), lower)
-
-        def send_picked(d, carry, i=i):
-            to = part_peer(d)
-            part_copy(
-                send_slots.at[i, to], recv_slots.at[i, part], slot_send.at[i], slot_recv.at[i], to
-            ).start()
-            return carry
-
-        lax.fori_loop(1, partners, send_picked, 0)
-        recv_slots[i, part] = send_slots[i, part]
-
-    for i in range(3):
-
-        def wait_picked(d, carry, i=i):
+                lower = picked[half:count, j * 128 : j * 128 + 128]
+                owner = tile * tile_owners + 2 * j
+                send_slots[n][owner] = jnp.where(left, upper, pltpu.roll(lower, 64, 1))
+                send_slots[n][owner + 1] = jnp.where(left, pltpu.roll(upper, 64, 1), lower)
+
+            def step(q, carry):
+                to = tile * tile_owners + q
+
+                @pl.when(to != part)
+                def _():
+                    slot_copy(n, to).start()
+
+                return carry
+
+            return lax.fori_loop(0, tile_owners, step, carry)
+
+        lax.fori_loop(0, tiles, pick, 0)
+        recv_slots[n][part] = send_slots[n][part]
+
+    def add_nodes(n):
+        i, start, count, _ = CHUNKS[n]
+
+        def arrive(d, carry):
             origin = part_peer(d)
             part_arrival(
-                recv_slots.at[i, origin], slot_send.at[i], slot_recv.at[i], origin
+                recv_slots[n].at[origin], slot_send.at[n], slot_recv.at[n], origin
             ).wait_recv()
             return carry
 
-        lax.fori_loop(1, partners, wait_picked, 0)
-        half = coefs // 2
+        lax.fori_loop(1, partners, arrive, 0)
         for j in range(pairs):
-            even = recv_slots[i, 2 * j]
-            odd = recv_slots[i, 2 * j + 1]
+            even = recv_slots[n][2 * j]
+            odd = recv_slots[n][2 * j + 1]
             upper = jnp.where(left, even, pltpu.roll(odd, 64, 1))
             lower = jnp.where(left, pltpu.roll(even, 64, 1), odd)
             high, low = split(jnp.concatenate([upper, lower], axis=0))
-            slot_parts[0:coefs, j * 128 : j * 128 + 128] = high
-            slot_parts[coefs : 2 * coefs, j * 128 : j * 128 + 128] = low
-        summed = dot(slot_parts[...], node_table[...])
-        totals[i] = summed[0:coefs] + summed[coefs : 2 * coefs]
-        store = pltpu.make_async_copy(totals.at[i], totals_hbm.at[i], store_sem.at[3 + i])
+            slot_parts[0:count, j * 128 : j * 128 + 128] = high
+            slot_parts[count : 2 * count, j * 128 : j * 128 + 128] = low
+        summed = dot(slot_parts[0 : 2 * count, :], node_table[...])
+        totals[i, start : start + count, :] = summed[0:count] + summed[count : 2 * count]
+        store = pltpu.make_async_copy(
+            totals.at[i, pl.ds(start, count)],
+            totals_hbm.at[i, pl.ds(start, count)],
+            store_sem.at[len(CHUNKS) + n],
+        )
         store.start()
         stores.append(store)
+
+    advect(0)
+    send_back(0)
+    send_back(1)
+    advect(1)
+    send_back(2)
+    send_picked(0)
+    send_picked(1)
+    advect(2)
+    for n in range(3, len(CHUNKS)):
+        send_back(n)
+    for n in range(2, len(CHUNKS)):
+        send_picked(n)
+    for n in range(len(CHUNKS)):
+        add_nodes(n)
 
     def sent_group(d, carry):
         to = group_peer(d)
         group_copy(stage_a.at[to], coef_a.at[me], a_send, a_recv, to, to).wait_send()
         group_copy(stage_b.at[to], coef_b.at[me], b_send, b_recv, to, to).wait_send()
-        for i in range(3):
-            group_copy(
-                send_adv.at[i, to], recv_adv.at[i, me], adv_send.at[i], adv_recv.at[i], to, to
-            ).wait_send()
+        for n in range(len(CHUNKS)):
+            back_copy(n, to).wait_send()
         return carry
 
     lax.fori_loop(1, groups, sent_group, 0)
@@ -507,10 +575,8 @@
     def sent_part(d, carry):
         to = part_peer(d)
         part_copy(nodes.at[to], node_in.at[part], node_send, node_recv, to).wait_send()
-        for i in range(3):
-            part_copy(
-                send_slots.at[i, to], recv_slots.at[i, part], slot_send.at[i], slot_recv.at[i], to
-            ).wait_send()
+        for n in range(len(CHUNKS)):
+            slot_copy(n, to).wait_send()
         return carry
 
     lax.fori_loop(1, partners, sent_part, 0)
@@ -525,21 +591,13 @@
     partners = lax.axis_size("elems")
     points = local_points // groups
     pairs = partners // 2
-    slot_count = send_point.shape[2]
     synth, analysis, slope, dz = spectral_tables(planes)
     synth_high, synth_low = halves_of(np.concatenate([synth, slope], axis=0))
     analysis_high, analysis_low = halves_of(analysis)
     grad = gradient_tables(points // (NP * NP), 256)
 
-    live = jnp.arange(slot_count, dtype=jnp.int32)[None, :] < pair_counts[0][:, None]
-    picks = jnp.where(live, send_point[0], -1).reshape(pairs, 2 * slot_count)
-    nodes = jnp.where(live, dest_node[0], -1).astype(F32)
-    nodes = jnp.concatenate([nodes, nodes], axis=1)[:, None, :]
-
     rows = -(-local_points // 128) * 128
     any_spec = pl.BlockSpec(memory_space=pl.ANY)
-    vmem_spec = pl.BlockSpec(memory_space=pltpu.VMEM)
-    smem_spec = pl.BlockSpec(memory_space=pltpu.SMEM)
 
     def room(*shape, dtype=F32):
         return pltpu.VMEM(shape, dtype)
@@ -547,7 +605,11 @@
     dma = pltpu.SemaphoreType.DMA
     scratch = [
         room(3, coefs, local_points),
-        room(3, 1, points, planes),
+        room(3, points, 1, planes),
+        pltpu.SMEM(metrics.shape, F32),
+        room(*send_point.shape, dtype=jnp.int32),
+        room(*dest_node.shape, dtype=jnp.int32),
+        pltpu.SMEM(pair_counts.shape, jnp.int32),
         room(2 * planes, planes, dtype=BF16),
         room(2 * planes, planes, dtype=BF16),
         room(planes, planes),
@@ -564,48 +626,52 @@
         room(3, planes, 512),
         room(256, 512, dtype=BF16),
         room(256, 512, dtype=BF16),
+        room(pairs, 128, dtype=jnp.int32),
+        room(partners, 1, 128),
         room(rows, pairs * 128, dtype=BF16),
         room(128, 128),
         room(pairs * 128, NODES_OWN, dtype=BF16),
         room(partners, 1, 128),
         room(3, planes, 256),
         room(3, planes, 256),
-        room(3, planes, 512),
+        room(planes, 512),
         room(planes, 256, dtype=BF16),
         room(planes, 256, dtype=BF16),
         room(planes, 256),
-        room(3, groups, coefs + 24, 128),
-        room(3, groups, coefs + 24, 128),
         room(3, coefs, local_points),
         room(2 * coefs, rows, dtype=BF16),
-        room(3, partners, coefs // 2, 128),
-        room(3, partners, coefs // 2, 128),
         room(2 * coefs, pairs * 128, dtype=BF16),
         room(3, coefs, NODES_OWN),
-        dma((8,)),
-        dma((6,)),
+        dma((12,)),
+        dma((2 * len(CHUNKS),)),
         dma((groups,)),
         dma((groups,)),
         dma((groups,)),
         dma((groups,)),
-        dma((3, groups)),
-        dma((3, groups)),
+        dma((len(CHUNKS), groups)),
+        dma((len(CHUNKS), groups)),
         dma((partners,)),
         dma((partners,)),
-        dma((3, partners)),
-        dma((3, partners)),
+        dma((len(CHUNKS), partners)),
+        dma((len(CHUNKS), partners)),
     ]
+    for _ in range(2):
+        for _, _, count, fold in CHUNKS:
+            scratch.append(room(groups, count + packed_rows(count, fold), 128))
+    for _ in range(2):
+        for _, _, count, _ in CHUNKS:
+            scratch.append(room(partners, count // 2, 128))
 
     def kernel(*refs):
         body(groups, partners, points, *refs)
 
-    return pl.pallas_call(
+    results = pl.pallas_call(
         kernel,
         out_shape=(
             jax.ShapeDtypeStruct((3, coefs, local_points), F32),
             jax.ShapeDtypeStruct((3, coefs, NODES_OWN), F32),
         ),
-        in_specs=[any_spec, any_spec, smem_spec, vmem_spec, vmem_spec] + [any_spec] * 6,
+        in_specs=[any_spec] * 12,
         out_specs=(any_spec, any_spec),
         scratch_shapes=scratch,
         compiler_params=pltpu.CompilerParams(
@@ -613,10 +679,11 @@
         ),
     )(
         adjoint_modes,
-        base_planes,
+        jnp.transpose(base_planes, (0, 2, 1, 3)),
         metrics,
-        picks,
-        nodes,
+        send_point,
+        dest_node,
+        pair_counts,
         synth_high,
         synth_low,
         jnp.asarray(dz, dtype=F32),
@@ -624,6 +691,35 @@
         analysis_low,
         grad,
     )
+
+    def hand_over(advection, totals, advection_out, totals_out, held, held_totals, sem_in, sem_out):
+        pieces = [
+            (advection.at[c], held.at[c], advection_out.at[c]) for c in range(components)
+        ] + [(totals, held_totals, totals_out)]
+        loads = [
+            pltpu.make_async_copy(source, middle, sem_in.at[i])
+            for i, (source, middle, _) in enumerate(pieces)
+        ]
+        stores = [
+            pltpu.make_async_copy(middle, target, sem_out.at[i])
+            for i, (_, middle, target) in enumerate(pieces)
+        ]
+        for load in loads:
+            load.start()
+        for load, store in zip(loads, stores):
+            load.wait()
+            store.start()
+        for store in stores:
+            store.wait()
+
+    return pl.pallas_call(
+        hand_over,
+        out_shape=tuple(jax.ShapeDtypeStruct(r.shape, r.dtype) for r in results),
+        in_specs=[any_spec, any_spec],
+        out_specs=(any_spec, any_spec),
+        scratch_shapes=[room(*r.shape) for r in results] + [dma((components + 1,))] * 2,
+        compiler_params=pltpu.CompilerParams(vmem_limit_bytes=56 * 1024 * 1024),
+    )(*results)
 
 
 def solution(mesh):

time: 90.3 us -> 77 us (0.85)
  local copies, waits for them, and re-layouts: 6.99 us -> 0 us
  Pallas kernels: 78.9 us -> 75.3 us
  other arithmetic: 3.39 us -> 0 us
    unnamed x6 -> x0, local copies, waits for them, and re-layouts: 5.86 us -> none
    pallas_call x1, Pallas kernels: 78.9 us -> 73.1 us  [per_device(): pl.pallas_call(kernel, out_shape=(jax.ShapeDtypeStruct((3, coefs, local_p...]
    pallas_call x0 -> x1, Pallas kernels: none -> 2.16 us  [per_device(): pl.pallas_call(hand_over, out_shape=tuple((jax.ShapeDtypeStruct(r.shape,...]
    unnamed x1 -> x0, other arithmetic: 1.32 us -> none
where the time goes in v1:
time: 77 us; the launch traced here: 75.9 us
  Pallas kernels  75.3 us (98%)
    pallas_call x1, Pallas kernels, per_device(): pl.pallas_call(kernel, out_shape=(jax.ShapeDtypeStruct((3, coefs, local_p...  73.1 us
    pallas_call x1, Pallas kernels, per_device(): pl.pallas_call(hand_over, out_shape=tuple((jax.ShapeDtypeStruct(r.shape,...  2.16 us

profile of v1, /device:TPU:1, one launch (start us, length us, event | category | flops | bytes accessed | tf_op | source)
XLA Modules:
  0.0 75.9 jit_solution(2347302621003152520)
XLA Ops:
  0.6 73.1 %shard_map.131 = (f32[3,64,1296]{2,1,0:T(8,128)}, f32[3,64,512]{2,1,0:T(8,128)}) custom-call(f32[3,64,1296]{2,1,0:T(8,128)} %refs_0_.1, f32[3,162,1,512]{3,2,1,0:T(1,128)} %bitcast.1, f32[4,16]{1,0:T(4,128)} %refs_2_.1, s32[1,32,64]{2,1,0:T(8,128)} %refs_3_.1, s32[1,32,64]{2,1,0:T(8,128)} %refs_4_.1, s32[1,32]{1,0:T(1,128)} %refs_5_.1, ...), custom_call_target="tpu_custom_call" | custom-call | tf_op jit(solution)/shard_map/pallas_call | solution.py:668
  73.8 2.2 %shard_map.132 = (f32[3,64,1296]{2,1,0:T(8,128)}, f32[3,64,512]{2,1,0:T(8,128)}) custom-call(f32[3,64,1296]{2,1,0:T(8,128)} %get-tuple-element.4.advection, f32[3,64,512]{2,1,0:T(8,128)} %get-tuple-element.5.totals), custom_call_target="tpu_custom_call" | custom-call | tf_op jit(solution)/shard_map/pallas_call | solution.py:715

commit v2 on v1

--- a/solution.py
+++ b/solution.py
@@ -14,7 +14,21 @@
 
 span_wavenumber = 0.4
 
-CHUNKS = ((0, 0, 16, 2), (0, 16, 48, 3), (1, 0, 64, 3), (2, 0, 64, 3))
+CHUNKS = ((0, 0, 64, 3, 16), (1, 0, 64, 3, 16), (2, 0, 64, 3, 16))
+
+RING = 8
+UP, DOWN, HERE = 0, 1, 2
+DISTANCES = (4, 3, 5, 2, 6, 1, 7, 0)
+
+
+def routes(distance):
+    if distance == 0:
+        return ((HERE, 0),)
+    if 2 * distance == RING:
+        return ((UP, distance - 1), (DOWN, distance - 1))
+    if 2 * distance < RING:
+        return ((UP, distance - 1),)
+    return ((DOWN, RING - distance - 1),)
 
 
 def packed_rows(count, fold):
@@ -149,6 +163,8 @@
     adv_parts,
     slot_parts,
     totals,
+    dense,
+    dense_in,
     load_sem,
     store_sem,
     a_send,
@@ -161,6 +177,8 @@
     node_recv,
     slot_send,
     slot_recv,
+    dense_send,
+    dense_recv,
     *chunk_rooms,
 ):
     send_adv, recv_adv, send_slots, recv_slots = (
@@ -173,25 +191,38 @@
     extra = points - 128
     pairs = partners // 2
     full = groups * points
+    side = partners // RING
+    level = part // side
+    column = lax.rem(part, side)
+    reach = RING // 2
+    blocks = 2 * reach * side + side
+
+    def device_at(steps, other):
+        return lax.rem(level + steps + RING, RING) * side + other
+
+    def block_at(way, steps, other):
+        return (way * reach + steps) * side + other
 
     barrier = pltpu.get_barrier_semaphore()
 
     def group_peer(d):
         return lax.rem(me + d, groups)
-
-    def part_peer(d):
-        return lax.rem(part + d, partners)
 
     def greet_group(d, carry):
         pl.semaphore_signal(barrier, inc=1, device_id=(group_peer(d), part), device_id_type=MESH)
         return carry
 
     def greet_part(d, carry):
-        pl.semaphore_signal(barrier, inc=1, device_id=(me, part_peer(d)), device_id_type=MESH)
+        to = device_at(d // side - reach + 1, lax.rem(d, side))
+
+        @pl.when(to != part)
+        def _():
+            pl.semaphore_signal(barrier, inc=1, device_id=(me, to), device_id_type=MESH)
+
         return carry
 
     lax.fori_loop(1, groups, greet_group, 0)
-    lax.fori_loop(1, partners, greet_part, 0)
+    lax.fori_loop(0, (2 * reach - 1) * side, greet_part, 0)
 
     loads = [
         pltpu.make_async_copy(source, target, load_sem.at[i])
@@ -212,52 +243,59 @@
             )
         )
     ]
-    for load in loads:
+    loads[0].start()
+
+    for n, (_, _, count, _, upward) in enumerate(CHUNKS):
+        for other in range(side):
+            if upward < count // 2:
+                recv_slots[n][block_at(UP, reach - 1, other), upward : count // 2, :] = jnp.zeros(
+                    (count // 2 - upward, 128), F32
+                )
+            if upward:
+                recv_slots[n][block_at(DOWN, reach - 1, other), 0:upward, :] = jnp.zeros(
+                    (upward, 128), F32
+                )
+    loads[0].wait()
+    for load in loads[1:]:
         load.start()
-
-    loads[0].wait()
     for g in range(groups):
         first = g * points
         stage_a[g, :, 0:128] = x_v[0, :, first : first + 128]
-        stage_a[g, :, 128:256] = x_v[1, :, first : first + 128]
-        stage_b[g, :, 0:128] = x_v[2, :, first : first + 128]
         rest = [x_v[c, :, first + 128 : first + points] for c in range(3)]
         rest.append(jnp.zeros((coefs, 128 - 3 * extra), F32))
-        stage_b[g, :, 128:256] = jnp.concatenate(rest, axis=1)
-
-    pl.semaphore_wait(barrier, groups - 1 + partners - 1)
-
-    def group_copy(source, target, send, recv, to, slot):
+        stage_a[g, :, 128:256] = jnp.concatenate(rest, axis=1)
+
+    pl.semaphore_wait(barrier, groups - 1 + (2 * reach - 1) * side - 1)
+
+    def group_copy(source, target, send, recv, to):
         return pltpu.make_async_remote_copy(
             src_ref=source,
             dst_ref=target,
-            send_sem=send.at[slot],
-            recv_sem=recv.at[me],
+            send_sem=send,
+            recv_sem=recv,
             device_id=(to, part),
             device_id_type=MESH,
         )
 
-    def group_arrival(target, send, recv, origin):
-        return pltpu.make_async_remote_copy(
-            src_ref=target,
-            dst_ref=target,
-            send_sem=send.at[origin],
-            recv_sem=recv.at[origin],
-            device_id=(origin, part),
-            device_id_type=MESH,
-        )
+    def group_all(room, send, recv):
+        whole = room.at[pl.ds(0, groups - 1)]
+        return group_copy(whole, whole, send, recv, me)
 
     def send_a(d, carry):
         to = group_peer(d)
-        group_copy(stage_a.at[to], coef_a.at[me], a_send, a_recv, to, to).start()
+        group_copy(stage_a.at[to], coef_a.at[me], a_send, a_recv, to).start()
         return carry
 
     def send_b(d, carry):
         to = group_peer(d)
-        group_copy(stage_b.at[to], coef_b.at[me], b_send, b_recv, to, to).start()
+        group_copy(stage_b.at[to], coef_b.at[me], b_send, b_recv, to).start()
         return carry
 
     lax.fori_loop(1, groups, send_a, 0)
+    for g in range(groups):
+        first = g * points
+        stage_b[g, :, 0:128] = x_v[1, :, first : first + 128]
+        stage_b[g, :, 128:256] = x_v[2, :, first : first + 128]
     lax.fori_loop(1, groups, send_b, 0)
     coef_a[me] = stage_a[me]
     coef_b[me] = stage_b[me]
@@ -273,8 +311,8 @@
     wanted = jnp.where(live, send_point[0], -1)
     fed = jnp.where(live, dest_node[0], -1).astype(F32)
     for o in range(partners):
-        side = o % 2 * 64
-        picks[o // 2 : o // 2 + 1, side : side + 64] = wanted[o : o + 1]
+        half = o % 2 * 64
+        picks[o // 2 : o // 2 + 1, half : half + 64] = wanted[o : o + 1]
         nodes[o, :, 0:64] = fed[o : o + 1]
         nodes[o, :, 64:128] = fed[o : o + 1]
 
@@ -282,29 +320,38 @@
         return pltpu.make_async_remote_copy(
             src_ref=source,
             dst_ref=target,
-            send_sem=send.at[to],
-            recv_sem=recv.at[part],
+            send_sem=send,
+            recv_sem=recv,
             device_id=(me, to),
             device_id_type=MESH,
         )
 
-    def part_arrival(target, send, recv, origin):
-        return pltpu.make_async_remote_copy(
-            src_ref=target,
-            dst_ref=target,
-            send_sem=send.at[origin],
-            recv_sem=recv.at[origin],
-            device_id=(me, origin),
-            device_id_type=MESH,
-        )
-
-    def send_nodes(d, carry):
-        to = part_peer(d)
-        part_copy(nodes.at[to], node_in.at[part], node_send, node_recv, to).start()
-        return carry
-
-    lax.fori_loop(1, partners, send_nodes, 0)
-    node_in[part] = nodes[part]
+    def each_other(steps, act):
+        def step(d, carry):
+            act(lax.rem(column + d, side))
+            return carry
+
+        lax.fori_loop(0 if steps else 1, side, step, 0)
+
+    def node_copy(way, steps, distance, other):
+        landed = block_at(way, steps, column)
+        to = device_at(-steps if way == DOWN else steps, other)
+        owner = device_at(distance, other)
+        return part_copy(
+            nodes.at[owner], node_in.at[landed], node_send, node_recv, to
+        )
+
+    node_whole = node_in.at[pl.ds(0, blocks - 3)]
+    node_all = part_copy(node_whole, node_whole, node_send, node_recv, part)
+
+    for distance in DISTANCES:
+        for way, steps in routes(distance):
+            each_other(
+                steps,
+                lambda other, w=way, s=steps, d=distance: node_copy(w, s, d, other).start(),
+            )
+            if steps == 0:
+                node_in[block_at(way, steps, column)] = nodes[device_at(distance, column)]
 
     for load in loads[4:8]:
         load.wait()
@@ -337,28 +384,26 @@
     rows = pick_table.shape[0]
     point_idx = lax.broadcasted_iota(jnp.int32, (rows, 128), 0)
 
-    def pick_step(j, carry):
-        wanted = picks[pl.ds(j, 1), :]
-        columns = pl.ds(pl.multiple_of(j * 128, 128), 128)
+    def pick_step(j, carry, place, distance):
+        wanted = picks[pl.ds(lax.rem(level + distance, RING) * (side // 2) + j, 1), :]
+        columns = pl.ds(pl.multiple_of((place * (side // 2) + j) * 128, 128), 128)
         pick_table[:, columns] = jnp.where(point_idx == wanted, 1.0, 0.0).astype(BF16)
         return carry
 
-    lax.fori_loop(0, pairs, pick_step, 0)
-
-    def wait_nodes(d, carry):
-        origin = part_peer(d)
-        part_arrival(node_in.at[origin], node_send, node_recv, origin).wait_recv()
-        return carry
-
-    lax.fori_loop(1, partners, wait_nodes, 0)
+    for place, distance in enumerate(DISTANCES):
+        lax.fori_loop(
+            0, side // 2, lambda j, c, p=place, d=distance: pick_step(j, c, p, d), 0
+        )
+
+    node_all.wait_recv()
     lane = lax.broadcasted_iota(jnp.int32, (1, 128), 1)
     left = lane < 64
     node_rows[...] = jnp.zeros((128, 128), F32)
-    for j in range(pairs):
+    for j in range(blocks // 2):
         node_rows[j : j + 1, :] = jnp.where(left, node_in[2 * j], node_in[2 * j + 1])
     node_columns = jnp.transpose(node_rows[...])
     node_idx = lax.broadcasted_iota(jnp.int32, (128, NODES_OWN), 1).astype(F32)
-    for j in range(pairs):
+    for j in range(blocks // 2):
         node_table[128 * j : 128 * j + 128, :] = jnp.where(
             node_idx == node_columns[:, j : j + 1], 1.0, 0.0
         ).astype(BF16)
@@ -367,29 +412,11 @@
     for load in loads[8:]:
         load.wait()
 
-    def wait_a(d, carry):
-        origin = group_peer(d)
-        group_arrival(coef_a.at[origin], a_send, a_recv, origin).wait_recv()
-        return carry
-
-    lax.fori_loop(1, groups, wait_a, 0)
+    group_all(coef_a, a_send, a_recv).wait_recv()
     high, low = split(coef_a[...].reshape(planes, 256))
     both = dot3(synth_high[...], synth_low[...], high, low)
     vel[0, :, 0:128] = both[0:planes, 0:128]
-    vel[1, :, 0:128] = both[0:planes, 128:256]
     along_z[0, :, 0:128] = both[planes : 2 * planes, 0:128]
-    along_z[1, :, 0:128] = both[planes : 2 * planes, 128:256]
-
-    def wait_b(d, carry):
-        origin = group_peer(d)
-        group_arrival(coef_b.at[origin], b_send, b_recv, origin).wait_recv()
-        return carry
-
-    lax.fori_loop(1, groups, wait_b, 0)
-    high, low = split(coef_b[...].reshape(planes, 256))
-    both = dot3(synth_high[...], synth_low[...], high, low)
-    vel[2, :, 0:128] = both[0:planes, 0:128]
-    along_z[2, :, 0:128] = both[planes : 2 * planes, 0:128]
     for c in range(3):
         rest = both[:, 128:256]
         if c:
@@ -397,6 +424,13 @@
         rest = jnp.where(lane < extra, rest, 0.0)
         vel[c, :, 128:256] = rest[0:planes]
         along_z[c, :, 128:256] = rest[planes : 2 * planes]
+
+    group_all(coef_b, b_send, b_recv).wait_recv()
+    high, low = split(coef_b[...].reshape(planes, 256))
+    both = dot3(synth_high[...], synth_low[...], high, low)
+    for c in (1, 2):
+        vel[c, :, 0:128] = both[0:planes, 128 * c - 128 : 128 * c]
+        along_z[c, :, 0:128] = both[planes : 2 * planes, 128 * c - 128 : 128 * c]
 
     block = 32
 
@@ -421,11 +455,11 @@
 
     def back_copy(n, to):
         return group_copy(
-            send_adv[n].at[to], recv_adv[n].at[me], adv_send.at[n], adv_recv.at[n], to, to
+            send_adv[n].at[to], recv_adv[n].at[me], adv_send.at[n], adv_recv.at[n], to
         )
 
     def send_back(n):
-        _, start, count, fold = CHUNKS[n]
+        _, start, count, fold, _ = CHUNKS[n]
         packed = packed_rows(count, fold)
         for m in range(groups):
             at = m * coefs + start
@@ -449,9 +483,45 @@
 
     stores = []
 
-    def slot_copy(n, to):
+    def way_rows(n, way, steps):
+        _, _, count, _, upward = CHUNKS[n]
+        if steps < reach - 1 or way == HERE:
+            return 0, count // 2
+        return (0, upward) if way == UP else (upward, count // 2 - upward)
+
+    def slot_copy(n, way, steps, distance, other):
+        first, rows_sent = way_rows(n, way, steps)
+        landed = block_at(way, steps, column)
+        place = DISTANCES.index(distance) * side + other
         return part_copy(
-            send_slots[n].at[to], recv_slots[n].at[part], slot_send.at[n], slot_recv.at[n], to
+            send_slots[n].at[place, pl.ds(first, rows_sent)],
+            recv_slots[n].at[landed, pl.ds(first, rows_sent)],
+            slot_send.at[n],
+            slot_recv.at[int(way == HERE), n],
+            device_at(-steps if way == DOWN else steps, other),
+        )
+
+    summed_here = 2 * (reach - 2) * side + side + 2 * (side - 1)
+
+    def slots_all(n, count, here):
+        whole = recv_slots[n].at[pl.ds(0, count)]
+        return part_copy(whole, whole, slot_send.at[n], slot_recv.at[here, n], part)
+
+    def each_slot_copy(n, distance, act):
+        for way, steps in routes(distance):
+            if way_rows(n, way, steps)[1]:
+                each_other(
+                    steps,
+                    lambda other, w=way, s=steps: act(slot_copy(n, w, s, distance, other)),
+                )
+
+    def dense_copy(n, way):
+        return part_copy(
+            dense.at[way, n, pl.ds(0, CHUNKS[n][2])],
+            dense_in.at[way, n, pl.ds(0, CHUNKS[n][2])],
+            dense_send.at[way, n],
+            dense_recv.at[way, n],
+            device_at(1 if way == UP else -1, column),
         )
 
     wide = min(512, 128 * pairs)
@@ -459,17 +529,10 @@
     tile_owners = 2 * (wide // 128)
 
     def send_picked(n):
-        i, start, count, fold = CHUNKS[n]
+        i, start, count, fold, _ = CHUNKS[n]
         packed = packed_rows(count, fold)
 
-        def arrive(d, carry):
-            origin = group_peer(d)
-            group_arrival(
-                recv_adv[n].at[origin], adv_send.at[n], adv_recv.at[n], origin
-            ).wait_recv()
-            return carry
-
-        lax.fori_loop(1, groups, arrive, 0)
+        group_all(recv_adv[n], adv_send.at[n], adv_recv.at[n]).wait_recv()
         for g in range(groups):
             first = g * points
             rest = recv_adv[n][g, count : count + packed, :]
@@ -492,44 +555,27 @@
         adv_parts[count : 2 * count, 0:full] = low
         half = count // 2
 
-        def pick(t, carry):
-            tile = lax.rem(part // tile_owners + t, tiles)
-            columns = pl.ds(pl.multiple_of(tile * wide, 128), wide)
-            picked = dot(adv_parts[0 : 2 * count, :], pick_table[:, columns])
+        for t in range(tiles):
+            picked = dot(adv_parts[0 : 2 * count, :], pick_table[:, t * wide : (t + 1) * wide])
             picked = picked[0:count] + picked[count : 2 * count]
             for j in range(wide // 128):
                 upper = picked[0:half, j * 128 : j * 128 + 128]
                 lower = picked[half:count, j * 128 : j * 128 + 128]
-                owner = tile * tile_owners + 2 * j
-                send_slots[n][owner] = jnp.where(left, upper, pltpu.roll(lower, 64, 1))
-                send_slots[n][owner + 1] = jnp.where(left, pltpu.roll(upper, 64, 1), lower)
-
-            def step(q, carry):
-                to = tile * tile_owners + q
-
-                @pl.when(to != part)
-                def _():
-                    slot_copy(n, to).start()
-
-                return carry
-
-            return lax.fori_loop(0, tile_owners, step, carry)
-
-        lax.fori_loop(0, tiles, pick, 0)
-        recv_slots[n][part] = send_slots[n][part]
-
-    def add_nodes(n):
-        i, start, count, _ = CHUNKS[n]
-
-        def arrive(d, carry):
-            origin = part_peer(d)
-            part_arrival(
-                recv_slots[n].at[origin], slot_send.at[n], slot_recv.at[n], origin
-            ).wait_recv()
-            return carry
-
-        lax.fori_loop(1, partners, arrive, 0)
-        for j in range(pairs):
+                place = t * tile_owners + 2 * j
+                send_slots[n][place] = jnp.where(left, upper, pltpu.roll(lower, 64, 1))
+                send_slots[n][place + 1] = jnp.where(left, pltpu.roll(upper, 64, 1), lower)
+            for place in range(t * tile_owners // side, (t + 1) * tile_owners // side):
+                distance = DISTANCES[place]
+                each_slot_copy(n, distance, lambda copy: copy.start())
+                for way, steps in routes(distance):
+                    if steps == 0:
+                        recv_slots[n][block_at(way, steps, column)] = send_slots[n][
+                            place * side + column
+                        ]
+
+    def sum_blocks(n, first, last):
+        count = CHUNKS[n][2]
+        for j in range(first // 2, last // 2):
             even = recv_slots[n][2 * j]
             odd = recv_slots[n][2 * j + 1]
             upper = jnp.where(left, even, pltpu.roll(odd, 64, 1))
@@ -537,8 +583,29 @@
             high, low = split(jnp.concatenate([upper, lower], axis=0))
             slot_parts[0:count, j * 128 : j * 128 + 128] = high
             slot_parts[count : 2 * count, j * 128 : j * 128 + 128] = low
-        summed = dot(slot_parts[0 : 2 * count, :], node_table[...])
-        totals[i, start : start + count, :] = summed[0:count] + summed[count : 2 * count]
+        summed = dot(
+            slot_parts[0 : 2 * count, 64 * first : 64 * last], node_table[64 * first : 64 * last, :]
+        )
+        return summed[0:count] + summed[count : 2 * count]
+
+    def pass_on(n):
+        count = CHUNKS[n][2]
+        slots_all(n, summed_here, 0).wait_recv()
+        for way in (UP, DOWN):
+            dense[way, n, 0:count, :] = sum_blocks(
+                n, way * reach * side, (way + 1) * reach * side
+            )
+            dense_copy(n, way).start()
+
+    def add_nodes(n):
+        i, start, count, _, _ = CHUNKS[n]
+        slots_all(n, side - 1, 1).wait_recv()
+        here = sum_blocks(n, 2 * reach * side, blocks)
+        for way in (UP, DOWN):
+            dense_copy(n, way).wait_recv()
+        totals[i, start : start + count, :] = (
+            here + dense_in[UP, n, 0:count, :] + dense_in[DOWN, n, 0:count, :]
+        )
         store = pltpu.make_async_copy(
             totals.at[i, pl.ds(start, count)],
             totals_hbm.at[i, pl.ds(start, count)],
@@ -549,37 +616,30 @@
 
     advect(0)
     send_back(0)
+    advect(1)
     send_back(1)
-    advect(1)
+    advect(2)
     send_back(2)
     send_picked(0)
     send_picked(1)
-    advect(2)
-    for n in range(3, len(CHUNKS)):
-        send_back(n)
-    for n in range(2, len(CHUNKS)):
-        send_picked(n)
+    send_picked(2)
+    pass_on(0)
+    pass_on(1)
+    add_nodes(0)
+    pass_on(2)
+    add_nodes(1)
+    add_nodes(2)
+
+    group_all(stage_a, a_send, a_recv).wait_send()
+    group_all(stage_b, b_send, b_recv).wait_send()
     for n in range(len(CHUNKS)):
-        add_nodes(n)
-
-    def sent_group(d, carry):
-        to = group_peer(d)
-        group_copy(stage_a.at[to], coef_a.at[me], a_send, a_recv, to, to).wait_send()
-        group_copy(stage_b.at[to], coef_b.at[me], b_send, b_recv, to, to).wait_send()
-        for n in range(len(CHUNKS)):
-            back_copy(n, to).wait_send()
-        return carry
-
-    lax.fori_loop(1, groups, sent_group, 0)
-
-    def sent_part(d, carry):
-        to = part_peer(d)
-        part_copy(nodes.at[to], node_in.at[part], node_send, node_recv, to).wait_send()
-        for n in range(len(CHUNKS)):
-            slot_copy(n, to).wait_send()
-        return carry
-
-    lax.fori_loop(1, partners, sent_part, 0)
+        group_all(send_adv[n], adv_send.at[n], adv_recv.at[n]).wait_send()
+    node_all.wait_send()
+    for n in range(len(CHUNKS)):
+        slots_all(n, summed_here + side - 1, 0).wait_send()
+    for n in range(len(CHUNKS)):
+        for way in (UP, DOWN):
+            dense_copy(n, way).wait_send()
     for store in stores:
         store.wait()
 
@@ -597,6 +657,7 @@
     grad = gradient_tables(points // (NP * NP), 256)
 
     rows = -(-local_points // 128) * 128
+    blocks = partners + partners // RING
     any_spec = pl.BlockSpec(memory_space=pl.ANY)
 
     def room(*shape, dtype=F32):
@@ -630,8 +691,8 @@
         room(partners, 1, 128),
         room(rows, pairs * 128, dtype=BF16),
         room(128, 128),
-        room(pairs * 128, NODES_OWN, dtype=BF16),
-        room(partners, 1, 128),
+        room(blocks * 64, NODES_OWN, dtype=BF16),
+        room(blocks, 1, 128),
         room(3, planes, 256),
         room(3, planes, 256),
         room(planes, 512),
@@ -640,27 +701,31 @@
         room(planes, 256),
         room(3, coefs, local_points),
         room(2 * coefs, rows, dtype=BF16),
-        room(2 * coefs, pairs * 128, dtype=BF16),
+        room(2 * coefs, blocks * 64, dtype=BF16),
         room(3, coefs, NODES_OWN),
+        room(2, len(CHUNKS), coefs, NODES_OWN),
+        room(2, len(CHUNKS), coefs, NODES_OWN),
         dma((12,)),
         dma((2 * len(CHUNKS),)),
-        dma((groups,)),
-        dma((groups,)),
-        dma((groups,)),
-        dma((groups,)),
-        dma((len(CHUNKS), groups)),
-        dma((len(CHUNKS), groups)),
-        dma((partners,)),
-        dma((partners,)),
-        dma((len(CHUNKS), partners)),
-        dma((len(CHUNKS), partners)),
+        dma,
+        dma,
+        dma,
+        dma,
+        dma((len(CHUNKS),)),
+        dma((len(CHUNKS),)),
+        dma,
+        dma,
+        dma((len(CHUNKS),)),
+        dma((2, len(CHUNKS))),
+        dma((2, len(CHUNKS))),
+        dma((2, len(CHUNKS))),
     ]
     for _ in range(2):
-        for _, _, count, fold in CHUNKS:
+        for _, _, count, fold, _ in CHUNKS:
             scratch.append(room(groups, count + packed_rows(count, fold), 128))
-    for _ in range(2):
-        for _, _, count, _ in CHUNKS:
-            scratch.append(room(partners, count // 2, 128))
+    for received in (False, True):
+        for _, _, count, _, _ in CHUNKS:
+            scratch.append(room(blocks if received else partners, count // 2, 128))
 
     def kernel(*refs):
         body(groups, partners, points, *refs)

time: 77 us -> 70.4 us (0.914); the launches traced: 75.9 us -> 70.3 us
  Pallas kernels: 75.3 us -> 69.5 us
    pallas_call x1, Pallas kernels: 73.1 us -> 67.3 us  [per_device(): pl.pallas_call(kernel, out_shape=(jax.ShapeDtypeStruct((3, coefs, local_p...]
where the time goes in v2:
time: 70.4 us; the launch traced here: 70.3 us
  Pallas kernels  69.5 us (99%)
  between operations  0.8 us (1%)
    pallas_call x1, Pallas kernels, per_device(): pl.pallas_call(kernel, out_shape=(jax.ShapeDtypeStruct((3, coefs, local_p...  67.3 us
    pallas_call x1, Pallas kernels, per_device(): pl.pallas_call(hand_over, out_shape=tuple((jax.ShapeDtypeStruct(r.shape,...  2.16 us

profile of v2, /device:TPU:1, one launch (start us, length us, event | category | flops | bytes accessed | tf_op | source)
XLA Modules:
  0.0 70.3 jit_solution(16668191926241639315)
XLA Ops:
  0.6 67.3 %shard_map.131 = (f32[3,64,1296]{2,1,0:T(8,128)}, f32[3,64,512]{2,1,0:T(8,128)}) custom-call(f32[3,64,1296]{2,1,0:T(8,128)} %refs_0_.1, f32[3,162,1,512]{3,2,1,0:T(1,128)} %bitcast.1, f32[4,16]{1,0:T(4,128)} %refs_2_.1, s32[1,32,64]{2,1,0:T(8,128)} %refs_3_.1, s32[1,32,64]{2,1,0:T(8,128)} %refs_4_.1, s32[1,32]{1,0:T(1,128)} %refs_5_.1, ...), custom_call_target="tpu_custom_call" | custom-call | tf_op jit(solution)/shard_map/pallas_call | solution.py:733
  68.0 2.2 %shard_map.132 = (f32[3,64,1296]{2,1,0:T(8,128)}, f32[3,64,512]{2,1,0:T(8,128)}) custom-call(f32[3,64,1296]{2,1,0:T(8,128)} %get-tuple-element.4.advection, f32[3,64,512]{2,1,0:T(8,128)} %get-tuple-element.5.totals), custom_call_target="tpu_custom_call" | custom-call | tf_op jit(solution)/shard_map/pallas_call | solution.py:780

commit v3 on v2

--- a/solution.py
+++ b/solution.py
@@ -14,7 +14,7 @@
 
 span_wavenumber = 0.4
 
-CHUNKS = ((0, 0, 64, 3, 16), (1, 0, 64, 3, 16), (2, 0, 64, 3, 16))
+CHUNKS = ((0, 0, 32, 2, 8), (0, 32, 32, 2, 8), (1, 0, 64, 3, 16), (2, 0, 64, 3, 16))
 
 RING = 8
 UP, DOWN, HERE = 0, 1, 2
@@ -29,6 +29,9 @@
     if 2 * distance < RING:
         return ((UP, distance - 1),)
     return ((DOWN, RING - distance - 1),)
+
+
+CUTS = 1
 
 
 def packed_rows(count, fold):
@@ -228,7 +231,11 @@
         pltpu.make_async_copy(source, target, load_sem.at[i])
         for i, (source, target) in enumerate(
             (
-                (x_hbm, x_v),
+                *(
+                    (x_hbm.at[c, pl.ds(r, 16)], x_v.at[c, pl.ds(r, 16)])
+                    for c in range(3)
+                    for r in range(0, coefs, 16)
+                ),
                 (send_point_hbm, send_point),
                 (dest_node_hbm, dest_node),
                 (pair_counts_hbm, pair_counts),
@@ -243,7 +250,9 @@
             )
         )
     ]
-    loads[0].start()
+    cuts = 3 * coefs // 16
+    for load in loads[:cuts]:
+        load.start()
 
     for n, (_, _, count, _, upward) in enumerate(CHUNKS):
         for other in range(side):
@@ -255,9 +264,11 @@
                 recv_slots[n][block_at(DOWN, reach - 1, other), 0:upward, :] = jnp.zeros(
                     (upward, 128), F32
                 )
-    loads[0].wait()
-    for load in loads[1:]:
+    for load in loads[:cuts]:
+        load.wait()
+    for load in loads[cuts:]:
         load.start()
+    loads = loads[cuts:]
     for g in range(groups):
         first = g * points
         stage_a[g, :, 0:128] = x_v[0, :, first : first + 128]
@@ -300,7 +311,7 @@
     coef_a[me] = stage_a[me]
     coef_b[me] = stage_b[me]
 
-    for load in loads[1:4]:
+    for load in loads[0:3]:
         load.wait()
     owner_idx = lax.broadcasted_iota(jnp.int32, (partners, 64), 0)
     slot_idx = lax.broadcasted_iota(jnp.int32, (partners, 64), 1)
@@ -353,7 +364,7 @@
             if steps == 0:
                 node_in[block_at(way, steps, column)] = nodes[device_at(distance, column)]
 
-    for load in loads[4:8]:
+    for load in loads[3:7]:
         load.wait()
     lane_points = lax.broadcasted_iota(jnp.int32, (1, 256), 1)
     first_elem = me * (points // (NP * NP))
@@ -409,7 +420,7 @@
         ).astype(BF16)
     adv_parts[:, rows - 128 : rows] = jnp.zeros((2 * coefs, 128), BF16)
 
-    for load in loads[8:]:
+    for load in loads[7:]:
         load.wait()
 
     group_all(coef_a, a_send, a_recv).wait_recv()
@@ -425,26 +436,47 @@
         vel[c, :, 128:256] = rest[0:planes]
         along_z[c, :, 128:256] = rest[planes : 2 * planes]
 
-    group_all(coef_b, b_send, b_recv).wait_recv()
-    high, low = split(coef_b[...].reshape(planes, 256))
-    both = dot3(synth_high[...], synth_low[...], high, low)
-    for c in (1, 2):
-        vel[c, :, 0:128] = both[0:planes, 128 * c - 128 : 128 * c]
-        along_z[c, :, 0:128] = both[planes : 2 * planes, 128 * c - 128 : 128 * c]
-
     block = 32
 
-    def advect(i):
+    def first_pass(i):
         high, low = split(vel[i])
         vel_xy[...] = dot3(high, low, grad_high[...], grad_low[...])
 
         def point_step(b, carry):
             at = pl.ds(pl.multiple_of(b * block, block), block)
-            total = jnp.zeros((block, 256), F32)
+            total = vel[i, at, :] * flow_back(i, i, at)
             for j in range(3):
                 slope = along_z[i, at, :] if j == 2 else vel_xy[at, j * 256 : j * 256 + 256]
-                back = base_z[j, at, :] if i == 2 else flow_xy[j, at, i * 256 : i * 256 + 256]
-                total = total - base_t[j, at, :] * slope + vel[j, at, :] * back
+                total = total - base_t[j, at, :] * slope
+            adv[at, :] = total
+            return carry
+
+        lax.fori_loop(0, planes // block, point_step, 0)
+
+    def flow_back(i, j, at):
+        return base_z[j, at, :] if i == 2 else flow_xy[j, at, i * 256 : i * 256 + 256]
+
+    first_pass(0)
+    group_all(coef_b, b_send, b_recv).wait_recv()
+
+    def second_half(rows, target):
+        high, low = split(coef_b[...].reshape(planes, 256))
+        part_b = dot3(synth_high[rows, :], synth_low[rows, :], high, low)
+        target[1, :, 0:128] = part_b[:, 0:128]
+        target[2, :, 0:128] = part_b[:, 128:256]
+
+    second_half(slice(0, planes), vel)
+
+    def advect(i):
+        if i:
+            first_pass(i)
+
+        def point_step(b, carry):
+            at = pl.ds(pl.multiple_of(b * block, block), block)
+            total = adv[at, :]
+            for j in range(3):
+                if j != i:
+                    total = total + vel[j, at, :] * flow_back(i, j, at)
             high, low = split(total)
             phys_high[at, :] = high
             phys_low[at, :] = low
@@ -482,6 +514,9 @@
         recv_adv[n][me] = send_adv[n][me]
 
     stores = []
+
+    def late_slopes():
+        second_half(slice(planes, 2 * planes), along_z)
 
     def way_rows(n, way, steps):
         _, _, count, _, upward = CHUNKS[n]
@@ -616,19 +651,24 @@
 
     advect(0)
     send_back(0)
+    send_back(1)
+    late_slopes()
     advect(1)
-    send_back(1)
-    advect(2)
     send_back(2)
     send_picked(0)
+    advect(2)
+    send_back(3)
     send_picked(1)
     send_picked(2)
+    send_picked(3)
     pass_on(0)
     pass_on(1)
+    pass_on(2)
+    pass_on(3)
     add_nodes(0)
-    pass_on(2)
     add_nodes(1)
     add_nodes(2)
+    add_nodes(3)
 
     group_all(stage_a, a_send, a_recv).wait_send()
     group_all(stage_b, b_send, b_recv).wait_send()
@@ -705,7 +745,7 @@
         room(3, coefs, NODES_OWN),
         room(2, len(CHUNKS), coefs, NODES_OWN),
         room(2, len(CHUNKS), coefs, NODES_OWN),
-        dma((12,)),
+        dma((11 + 3 * coefs // 16,)),
         dma((2 * len(CHUNKS),)),
         dma,
         dma,
@@ -759,8 +799,11 @@
 
     def hand_over(advection, totals, advection_out, totals_out, held, held_totals, sem_in, sem_out):
         pieces = [
-            (advection.at[c], held.at[c], advection_out.at[c]) for c in range(components)
-        ] + [(totals, held_totals, totals_out)]
+            tuple(room.at[c, pl.ds(r, coefs // CUTS)] for room in rooms)
+            for rooms in ((advection, held, advection_out), (totals, held_totals, totals_out))
+            for c in range(components)
+            for r in range(0, coefs, coefs // CUTS)
+        ]
         loads = [
             pltpu.make_async_copy(source, middle, sem_in.at[i])
             for i, (source, middle, _) in enumerate(pieces)
@@ -782,7 +825,7 @@
         out_shape=tuple(jax.ShapeDtypeStruct(r.shape, r.dtype) for r in results),
         in_specs=[any_spec, any_spec],
         out_specs=(any_spec, any_spec),
-        scratch_shapes=[room(*r.shape) for r in results] + [dma((components + 1,))] * 2,
+        scratch_shapes=[room(*r.shape) for r in results] + [dma((2 * components * CUTS,))] * 2,
         compiler_params=pltpu.CompilerParams(vmem_limit_bytes=56 * 1024 * 1024),
     )(*results)
 

time: 70.4 us -> 68.7 us (0.976)
  Pallas kernels: 69.5 us -> 67.8 us
    pallas_call x1, Pallas kernels: 67.3 us -> 65.6 us  [per_device(): pl.pallas_call(kernel, out_shape=(jax.ShapeDtypeStruct((3, coefs, local_p...]
where the time goes in v3:
time: 68.7 us; the launch traced here: 68.6 us
  Pallas kernels  67.8 us (99%)
  between operations  0.8 us (1%)
    pallas_call x1, Pallas kernels, per_device(): pl.pallas_call(kernel, out_shape=(jax.ShapeDtypeStruct((3, coefs, local_p...  65.6 us
    pallas_call x1, Pallas kernels, per_device(): pl.pallas_call(hand_over, out_shape=tuple((jax.ShapeDtypeStruct(r.shape,...  2.19 us

profile of v3, /device:TPU:1, one launch (start us, length us, event | category | flops | bytes accessed | tf_op | source)
XLA Modules:
  0.0 68.6 jit_solution(8016474162876789529)
XLA Ops:
  0.6 65.6 %shard_map.131 = (f32[3,64,1296]{2,1,0:T(8,128)}, f32[3,64,512]{2,1,0:T(8,128)}) custom-call(f32[3,64,1296]{2,1,0:T(8,128)} %refs_0_.1, f32[3,162,1,512]{3,2,1,0:T(1,128)} %bitcast.1, f32[4,16]{1,0:T(4,128)} %refs_2_.1, s32[1,32,64]{2,1,0:T(8,128)} %refs_3_.1, s32[1,32,64]{2,1,0:T(8,128)} %refs_4_.1, s32[1,32]{1,0:T(1,128)} %refs_5_.1, ...), custom_call_target="tpu_custom_call" | custom-call | tf_op jit(solution)/shard_map/pallas_call | solution.py:773
  66.2 2.2 %shard_map.132 = (f32[3,64,1296]{2,1,0:T(8,128)}, f32[3,64,512]{2,1,0:T(8,128)}) custom-call(f32[3,64,1296]{2,1,0:T(8,128)} %get-tuple-element.4.advection, f32[3,64,512]{2,1,0:T(8,128)} %get-tuple-element.5.totals), custom_call_target="tpu_custom_call" | custom-call | tf_op jit(solution)/shard_map/pallas_call | solution.py:823

commit v4 on v3

--- a/solution.py
+++ b/solution.py
@@ -182,6 +182,8 @@
     slot_recv,
     dense_send,
     dense_recv,
+    ready_sem,
+    go_sem,
     *chunk_rooms,
 ):
     send_adv, recv_adv, send_slots, recv_slots = (
@@ -212,7 +214,12 @@
         return lax.rem(me + d, groups)
 
     def greet_group(d, carry):
-        pl.semaphore_signal(barrier, inc=1, device_id=(group_peer(d), part), device_id_type=MESH)
+        to = group_peer(d)
+
+        @pl.when(to != 0)
+        def _():
+            pl.semaphore_signal(barrier, inc=1, device_id=(to, part), device_id_type=MESH)
+
         return carry
 
     def greet_part(d, carry):
@@ -220,12 +227,16 @@
 
         @pl.when(to != part)
         def _():
-            pl.semaphore_signal(barrier, inc=1, device_id=(me, to), device_id_type=MESH)
+            pl.semaphore_signal(barrier, inc=1, device_id=(0, to), device_id_type=MESH)
 
         return carry
 
+    def tell_group(d, carry):
+        pl.semaphore_signal(go_sem, inc=1, device_id=(d, part), device_id_type=MESH)
+        return carry
+
+    others_near = (2 * reach - 1) * side - 1
     lax.fori_loop(1, groups, greet_group, 0)
-    lax.fori_loop(0, (2 * reach - 1) * side, greet_part, 0)
 
     loads = [
         pltpu.make_async_copy(source, target, load_sem.at[i])
@@ -276,7 +287,15 @@
         rest.append(jnp.zeros((coefs, 128 - 3 * extra), F32))
         stage_a[g, :, 128:256] = jnp.concatenate(rest, axis=1)
 
-    pl.semaphore_wait(barrier, groups - 1 + (2 * reach - 1) * side - 1)
+    @pl.when(me != 0)
+    def _():
+        pl.semaphore_wait(barrier, groups - 1)
+        pl.semaphore_signal(ready_sem, inc=1, device_id=(0, part), device_id_type=MESH)
+
+    @pl.when(me == 0)
+    def _():
+        pl.semaphore_wait(ready_sem, groups - 1)
+        lax.fori_loop(0, others_near + 1, greet_part, 0)
 
     def group_copy(source, target, send, recv, to):
         return pltpu.make_async_remote_copy(
@@ -355,6 +374,57 @@
     node_whole = node_in.at[pl.ds(0, blocks - 3)]
     node_all = part_copy(node_whole, node_whole, node_send, node_recv, part)
 
+    for load in loads[3:7]:
+        load.wait()
+    lane_points = lax.broadcasted_iota(jnp.int32, (1, 256), 1)
+    first_elem = me * (points // (NP * NP))
+
+    def metric_row(r):
+        row = jnp.zeros((1, 256), F32)
+        for e in range(points // (NP * NP)):
+            row = jnp.where(lane_points >= e * NP * NP, metrics[r, first_elem + e], row)
+        return row
+
+    for half in range(2):
+        grad = grad_tables[0] * metric_row(2 * half) + grad_tables[1] * metric_row(2 * half + 1)
+        high, low = split(grad)
+        grad_high[:, half * 256 : half * 256 + 256] = high
+        grad_low[:, half * 256 : half * 256 + 256] = low
+        vel_xy[0:256, half * 256 : half * 256 + 256] = grad
+    padded[128:256, :] = jnp.zeros((128, planes), F32)
+
+    def base_step(c, carry):
+        padded[0:points, :] = base_v[c, :, 0, :]
+        base_t[c] = jnp.transpose(padded[...])
+        base_z[c] = dot6(dz[...], base_t[c])
+        flow_xy[c] = dot6(base_t[c], vel_xy[0:256, :])
+        return carry
+
+    lax.fori_loop(0, 3, base_step, 0)
+
+    rows = pick_table.shape[0]
+    point_idx = lax.broadcasted_iota(jnp.int32, (rows, 128), 0)
+
+    def pick_step(j, carry, place, distance):
+        wanted = picks[pl.ds(lax.rem(level + distance, RING) * (side // 2) + j, 1), :]
+        columns = pl.ds(pl.multiple_of((place * (side // 2) + j) * 128, 128), 128)
+        pick_table[:, columns] = jnp.where(point_idx == wanted, 1.0, 0.0).astype(BF16)
+        return carry
+
+    for place, distance in enumerate(DISTANCES):
+        lax.fori_loop(
+            0, side // 2, lambda j, c, p=place, d=distance: pick_step(j, c, p, d), 0
+        )
+
+    @pl.when(me == 0)
+    def _():
+        pl.semaphore_wait(barrier, others_near)
+        lax.fori_loop(1, groups, tell_group, 0)
+
+    @pl.when(me != 0)
+    def _():
+        pl.semaphore_wait(go_sem, 1)
+
     for distance in DISTANCES:
         for way, steps in routes(distance):
             each_other(
@@ -364,60 +434,8 @@
             if steps == 0:
                 node_in[block_at(way, steps, column)] = nodes[device_at(distance, column)]
 
-    for load in loads[3:7]:
-        load.wait()
-    lane_points = lax.broadcasted_iota(jnp.int32, (1, 256), 1)
-    first_elem = me * (points // (NP * NP))
-
-    def metric_row(r):
-        row = jnp.zeros((1, 256), F32)
-        for e in range(points // (NP * NP)):
-            row = jnp.where(lane_points >= e * NP * NP, metrics[r, first_elem + e], row)
-        return row
-
-    for half in range(2):
-        grad = grad_tables[0] * metric_row(2 * half) + grad_tables[1] * metric_row(2 * half + 1)
-        high, low = split(grad)
-        grad_high[:, half * 256 : half * 256 + 256] = high
-        grad_low[:, half * 256 : half * 256 + 256] = low
-        vel_xy[0:256, half * 256 : half * 256 + 256] = grad
-    padded[128:256, :] = jnp.zeros((128, planes), F32)
-
-    def base_step(c, carry):
-        padded[0:points, :] = base_v[c, :, 0, :]
-        base_t[c] = jnp.transpose(padded[...])
-        base_z[c] = dot6(dz[...], base_t[c])
-        flow_xy[c] = dot6(base_t[c], vel_xy[0:256, :])
-        return carry
-
-    lax.fori_loop(0, 3, base_step, 0)
-
-    rows = pick_table.shape[0]
-    point_idx = lax.broadcasted_iota(jnp.int32, (rows, 128), 0)
-
-    def pick_step(j, carry, place, distance):
-        wanted = picks[pl.ds(lax.rem(level + distance, RING) * (side // 2) + j, 1), :]
-        columns = pl.ds(pl.multiple_of((place * (side // 2) + j) * 128, 128), 128)
-        pick_table[:, columns] = jnp.where(point_idx == wanted, 1.0, 0.0).astype(BF16)
-        return carry
-
-    for place, distance in enumerate(DISTANCES):
-        lax.fori_loop(
-            0, side // 2, lambda j, c, p=place, d=distance: pick_step(j, c, p, d), 0
-        )
-
-    node_all.wait_recv()
     lane = lax.broadcasted_iota(jnp.int32, (1, 128), 1)
     left = lane < 64
-    node_rows[...] = jnp.zeros((128, 128), F32)
-    for j in range(blocks // 2):
-        node_rows[j : j + 1, :] = jnp.where(left, node_in[2 * j], node_in[2 * j + 1])
-    node_columns = jnp.transpose(node_rows[...])
-    node_idx = lax.broadcasted_iota(jnp.int32, (128, NODES_OWN), 1).astype(F32)
-    for j in range(blocks // 2):
-        node_table[128 * j : 128 * j + 128, :] = jnp.where(
-            node_idx == node_columns[:, j : j + 1], 1.0, 0.0
-        ).astype(BF16)
     adv_parts[:, rows - 128 : rows] = jnp.zeros((2 * coefs, 128), BF16)
 
     for load in loads[7:]:
@@ -623,6 +641,18 @@
         )
         return summed[0:count] + summed[count : 2 * count]
 
+    def fill_node_table():
+        node_all.wait_recv()
+        node_rows[...] = jnp.zeros((128, 128), F32)
+        for j in range(blocks // 2):
+            node_rows[j : j + 1, :] = jnp.where(left, node_in[2 * j], node_in[2 * j + 1])
+        node_columns = jnp.transpose(node_rows[...])
+        node_idx = lax.broadcasted_iota(jnp.int32, (128, NODES_OWN), 1).astype(F32)
+        for j in range(blocks // 2):
+            node_table[128 * j : 128 * j + 128, :] = jnp.where(
+                node_idx == node_columns[:, j : j + 1], 1.0, 0.0
+            ).astype(BF16)
+
     def pass_on(n):
         count = CHUNKS[n][2]
         slots_all(n, summed_here, 0).wait_recv()
@@ -661,6 +691,7 @@
     send_picked(1)
     send_picked(2)
     send_picked(3)
+    fill_node_table()
     pass_on(0)
     pass_on(1)
     pass_on(2)
@@ -759,6 +790,8 @@
         dma((2, len(CHUNKS))),
         dma((2, len(CHUNKS))),
         dma((2, len(CHUNKS))),
+        pltpu.SemaphoreType.REGULAR,
+        pltpu.SemaphoreType.REGULAR,
     ]
     for _ in range(2):
         for _, _, count, fold, _ in CHUNKS:

time: 68.7 us -> 68.2 us (level)
  no operation moved by 1% of the time
where the time goes in v4:
time: 68.2 us; the launch traced here: 68 us
  Pallas kernels  67.2 us (99%)
  between operations  0.8 us (1%)
    pallas_call x1, Pallas kernels, per_device(): pl.pallas_call(kernel, out_shape=(jax.ShapeDtypeStruct((3, coefs, local_p...  65 us
    pallas_call x1, Pallas kernels, per_device(): pl.pallas_call(hand_over, out_shape=tuple((jax.ShapeDtypeStruct(r.shape,...  2.19 us

profile of v4, /device:TPU:1, one launch (start us, length us, event | category | flops | bytes accessed | tf_op | source)
XLA Modules:
  0.0 68.0 jit_solution(7209610736473181936)
XLA Ops:
  0.6 65.0 %shard_map.131 = (f32[3,64,1296]{2,1,0:T(8,128)}, f32[3,64,512]{2,1,0:T(8,128)}) custom-call(f32[3,64,1296]{2,1,0:T(8,128)} %refs_0_.1, f32[3,162,1,512]{3,2,1,0:T(1,128)} %bitcast.1, f32[4,16]{1,0:T(4,128)} %refs_2_.1, s32[1,32,64]{2,1,0:T(8,128)} %refs_3_.1, s32[1,32,64]{2,1,0:T(8,128)} %refs_4_.1, s32[1,32]{1,0:T(1,128)} %refs_5_.1, ...), custom_call_target="tpu_custom_call" | custom-call | tf_op jit(solution)/shard_map/pallas_call | solution.py:806
  65.7 2.2 %shard_map.132 = (f32[3,64,1296]{2,1,0:T(8,128)}, f32[3,64,512]{2,1,0:T(8,128)}) custom-call(f32[3,64,1296]{2,1,0:T(8,128)} %get-tuple-element.4.advection, f32[3,64,512]{2,1,0:T(8,128)} %get-tuple-element.5.totals), custom_call_target="tpu_custom_call" | custom-call | tf_op jit(solution)/shard_map/pallas_call | solution.py:856
